TPU v7x, 256 devices: a whole 4x4x8 slice. The times are simulated.
256 devices in a mesh: gx: 8 (over z), gy: 8 (over y, core), gz: 4 (over x).
Axes of the slice: x: 4, y: 4, z: 8, core: 2. Of those that a mesh axis runs over, the one named last changes fastest.
Arguments:
- source_term: float32 [128, 256, 512], P('gx', 'gy', 'gz'), may hold values from -9 to 9
- alpha_cell: float32 [128, 256, 512], P('gx', 'gy', 'gz'), may hold values from 0.5 to 2
- beta_x: float32 [128, 256, 512], P('gx', 'gy', 'gz'), may hold values from 4 to 40
- beta_y: float32 [128, 256, 512], P('gx', 'gy', 'gz'), may hold values from 4 to 40
- beta_z: float32 [128, 256, 512], P('gx', 'gy', 'gz'), may hold values from 4 to 40
Outputs:
- iterate_fine: float32 [128, 256, 512], P('gx', 'gy', 'gz')
- iterate_one: float32 [64, 128, 256], P('gx', 'gy', 'gz')
- iterate_two: float32 [32, 64, 128], P('gx', 'gy', 'gz')
- iterate_three: float32 [16, 32, 64], P('gx', 'gy', 'gz')
- bottom_source: float32 [8, 16, 32], replicated
All inputs are finite; a program needn't handle non-finite values.
Results may differ from a plain program's by a relative error of at most 0.00011.
Values sent between devices are 32-bit elements; how exact they have to be, the bound alone decides.
A program may use at most 128 MiB of HBM per device.

v0:
```python
import jax
import jax.numpy as jnp
from jax import lax
from jax.sharding import PartitionSpec as P

AGG = 3
SWEEPS = 4


spectrum_low = 0.25
spectrum_high = 2.0


def padded(cells, sides, width):
    for axis, dim in sides:
        count = lax.axis_size(axis)
        ends = count - 1
        head = lax.slice_in_dim(cells, 0, width, axis=dim)
        tail = lax.slice_in_dim(cells, cells.shape[dim] - width, cells.shape[dim], axis=dim)
        cells = jnp.concatenate(
            [
                lax.ppermute(tail, axis, [(i, (i + 1) % count) for i in range(ends)]),
                cells,
                lax.ppermute(head, axis, [((i + 1) % count, i) for i in range(ends)]),
            ],
            axis=dim,
        )
    return cells


def shifted(value, axis, steps):
    count = lax.axis_size(axis)
    initial, last = (max(0, -steps), min(count, count - steps))
    return lax.ppermute(value, axis, [(source, source + steps) for source in range(initial, last)])


def chebyshev_weights(count):
    middle = 0.5 * (spectrum_high + spectrum_low)
    spread = 0.5 * (spectrum_high - spectrum_low)
    sharpness = middle / spread
    weights = [(0.0, 1.0 / middle)]
    rho_prev = 1.0 / sharpness
    for sweep_index in range(1, count):
        rho_next = 1.0 / (2.0 * sharpness - rho_prev)
        weights.append((rho_next * rho_prev, 2.0 * rho_next / spread))
        rho_prev = rho_next
    return weights


def interior(field_values):
    return field_values[1:-1, 1:-1, 1:-1]


def neighbours(current, face_betas):
    face_x, face_y, face_z = face_betas
    summed = (
        interior(face_x) * current[:-2, 1:-1, 1:-1]
        + face_x[2:, 1:-1, 1:-1] * current[2:, 1:-1, 1:-1]
    )
    summed = summed + (
        interior(face_y) * current[1:-1, :-2, 1:-1]
        + face_y[1:-1, 2:, 1:-1] * current[1:-1, 2:, 1:-1]
    )
    summed = summed + (
        interior(face_z) * current[1:-1, 1:-1, :-2]
        + face_z[1:-1, 1:-1, 2:] * current[1:-1, 1:-1, 2:]
    )
    return summed


def diagonal(alpha_values, face_betas, level_scale):
    face_x, face_y, face_z = face_betas
    face_sum = (
        interior(face_x) + face_x[2:, 1:-1, 1:-1] + (interior(face_y) + face_y[1:-1, 2:, 1:-1])
    )
    face_sum = face_sum + (interior(face_z) + face_z[1:-1, 1:-1, 2:])
    return alpha_values + level_scale * face_sum


def apply_operator(current, face_betas, center_weight, level_scale):
    return center_weight * interior(current) - level_scale * neighbours(current, face_betas)


def chebyshev_sweep(
    current, older, face_betas, source, center_weight, inverse, level_scale, momentum, step_weight
):
    middle = interior(current)
    update = source - apply_operator(current, face_betas, center_weight, level_scale)
    return middle + momentum * (middle - older) + step_weight * inverse * update


def coarsen_cells(field_values):
    span_x, span_y, span_z = field_values.shape
    grouped = field_values.reshape(span_x // 2, 2, span_y // 2, 2, span_z // 2, 2)
    return jnp.mean(grouped, axis=(1, 3, 5))


def coarsen_faces(face_values, normal_dim):
    if normal_dim == 0:
        even_faces = face_values[0::2]
        span_x, span_y, span_z = even_faces.shape
        return jnp.mean(even_faces.reshape(span_x, span_y // 2, 2, span_z // 2, 2), axis=(2, 4))
    if normal_dim == 1:
        even_faces = face_values[:, 0::2]
        span_x, span_y, span_z = even_faces.shape
        return jnp.mean(even_faces.reshape(span_x // 2, 2, span_y, span_z // 2, 2), axis=(1, 4))
    even_faces = face_values[:, :, 0::2]
    span_x, span_y, span_z = even_faces.shape
    return jnp.mean(even_faces.reshape(span_x // 2, 2, span_y // 2, 2, span_z), axis=(1, 3))


def rim_iterate(field_values):
    return padded(field_values, (("gx", 0), ("gy", 1), ("gz", 2)), 1)


def next_faces(layer_x, layer_y, layer_z):
    above_x = shifted(layer_x, "gx", -1)
    above_y = shifted(layer_y, "gy", -1)
    above_z = shifted(layer_z, "gz", -1)
    return (above_x, above_y, above_z)


def extend_faces(face_betas, above, outer):
    face_x = jnp.pad(
        jnp.concatenate((face_betas[0], above[0]), 0), ((outer, 0), (outer, outer), (outer, outer))
    )
    face_y = jnp.pad(
        jnp.concatenate((face_betas[1], above[1]), 1), ((outer, outer), (outer, 0), (outer, outer))
    )
    face_z = jnp.pad(
        jnp.concatenate((face_betas[2], above[2]), 2), ((outer, outer), (outer, outer), (outer, 0))
    )
    return (face_x, face_y, face_z)


def single_level(source, alpha_values, face_betas, level_scale, weights):
    above = next_faces(face_betas[0][0:1], face_betas[1][:, 0:1], face_betas[2][:, :, 0:1])
    padded_betas = extend_faces(face_betas, above, 1)
    center_weight = diagonal(alpha_values, padded_betas, level_scale)
    inverse = 1.0 / center_weight
    older = jnp.zeros(source.shape, jnp.float32)
    current = weights[0][1] * inverse * source
    for sweep_index in range(1, SWEEPS):
        momentum, step_weight = weights[sweep_index]
        newer = chebyshev_sweep(
            rim_iterate(current),
            older,
            padded_betas,
            source,
            center_weight,
            inverse,
            level_scale,
            momentum,
            step_weight,
        )
        older = current
        current = newer
    residual = source - apply_operator(
        rim_iterate(current), padded_betas, center_weight, level_scale
    )
    return (current, residual)


def distributed_level(source, alpha_values, face_betas, level_scale, weights):
    return single_level(source, alpha_values, face_betas, level_scale, weights)


def tile_blocks(gathered):
    count_x = lax.axis_size("gx")
    count_y = lax.axis_size("gy")
    count_z = lax.axis_size("gz")
    layers = gathered.shape[1]
    span_x, span_y, span_z = (gathered.shape[2], gathered.shape[3], gathered.shape[4])
    grid_blocks = gathered.reshape(count_x, count_y, count_z, layers, span_x, span_y, span_z)
    grid_blocks = jnp.transpose(grid_blocks, (3, 0, 4, 1, 5, 2, 6))
    return grid_blocks.reshape(layers, count_x * span_x, count_y * span_y, count_z * span_z)


def coarsen_all(alpha_values, face_betas):
    coarse_betas = (
        coarsen_faces(face_betas[0], 0),
        coarsen_faces(face_betas[1], 1),
        coarsen_faces(face_betas[2], 2),
    )
    return (coarsen_cells(alpha_values), coarse_betas)


def body(source_term, alpha_cell, beta_x, beta_y, beta_z):
    weights = chebyshev_weights(SWEEPS)
    source = source_term
    alpha_values = alpha_cell
    face_betas = (beta_x, beta_y, beta_z)
    iterates = []
    for level_index in range(AGG):
        iterate, residual = distributed_level(
            source, alpha_values, face_betas, 0.25**level_index, weights
        )
        iterates.append(iterate)
        source = coarsen_cells(residual)
        alpha_values, face_betas = coarsen_all(alpha_values, face_betas)
    level_index = 3
    iterate, residual = distributed_level(
        source, alpha_values, face_betas, 0.25**level_index, weights
    )
    iterates.append(iterate)
    source = coarsen_cells(residual)
    gathered = lax.all_gather(source[None, None], ("gx", "gy", "gz"), axis=0, tiled=True)
    bottom_source = tile_blocks(gathered)[0]
    return (iterates[0], iterates[1], iterates[2], iterates[3], bottom_source)


def solution(mesh):
    return jax.shard_map(
        body,
        mesh=mesh,
        in_specs=(
            P("gx", "gy", "gz"),
            P("gx", "gy", "gz"),
            P("gx", "gy", "gz"),
            P("gx", "gy", "gz"),
            P("gx", "gy", "gz"),
        ),
        out_specs=(
            P("gx", "gy", "gz"),
            P("gx", "gy", "gz"),
            P("gx", "gy", "gz"),
            P("gx", "gy", "gz"),
            P(),
        ),
        check_vma=False,
    )
```

profile of v0, /device:TPU:1, one launch (start us, length us, event | category | flops | bytes accessed | tf_op | source)
XLA Modules:
  0.0 567.5 jit_solution(16596935560975034157)
XLA Ops:
  3.5 5.1 collective-permute-start.1
  10.1 8.8 %collective-permute-done.2 = f32[16,32,1]{2,1,0:T(8,128)S(1)} collective-permute-done((f32[16,32,1]{2,1,0:T(8,128)}, f32[16,32,1]{2,1,0:T(8,128)S(1)}, u32[]{:S(2)}, u32[]{:S(2)}) %collective-permute-start.2) | collective-permute-done | bytes 2080 | tf_op jit(solution)/shard_map/ppermute | solution.py:34
  22.2 4.9 collective-permute-start.3
  35.9 4.0 collective-permute-start.7
  39.9 6.8 %collective-permute-done.8 = f32[18,34,1]{2,1,0:T(8,128)S(1)} collective-permute-done((f32[18,34,1]{2,1,0:T(8,128)S(1)}, f32[18,34,1]{2,1,0:T(8,128)S(1)}, u32[]{:S(2)}, u32[]{:S(2)}) %collective-permute-start.8) | collective-permute-done | bytes 2480 | tf_op jit(solution)/shard_map/ppermute | solution.py:24
  49.4 4.3 collective-permute-start.9
  54.5 4.0 collective-permute-start.12
  63.4 4.8 collective-permute-start.13
  68.2 7.1 %collective-permute-done.14 = f32[18,34,1]{2,1,0:T(8,128)S(1)} collective-permute-done((f32[18,34,1]{2,1,0:T(8,128)S(1)}, f32[18,34,1]{2,1,0:T(8,128)S(1)}, u32[]{:S(2)}, u32[]{:S(2)}) %collective-permute-start.14) | collective-permute-done | bytes 2480 | tf_op jit(solution)/shard_map/ppermute | solution.py:24
  78.1 4.5 collective-permute-start.15
  92.8 4.8 collective-permute-start.19
  97.5 6.3 %slice.951 = f32[16,32,64]{2,1,0:T(8,128)S(1)} slice(f32[16,32,128]{2,1,0:T(8,128)S(1)} %copy-done.1), slice={[0:16:1], [0:32:1], [0:128:2]} | slice | bytes 262144 | tf_op jit(solution)/shard_map/slice | solution.py:107
  108.5 4.8 collective-permute-start.24
  134.2 5.3 collective-permute-start.28
  141.1 18.1 %reshape.75 = f32[8,2,16,2,64,2]{5,4,3,2,1,0:T(8,128)} reshape(f32[16,32,128]{2,1,0:T(8,128)S(1)} %copy-done) | data formatting | bytes 524288 | tf_op jit(solution)/shard_map/reshape | solution.py:94
  159.2 7.1 %reduce_sum.151 = f32[8,16,64]{2,1,0:T(8,128)S(1)} reduce(f32[8,2,16,2,64,2]{5,4,3,2,1,0:T(8,128)} %reshape.75, f32[]{:T(128)} %constant.24.clone.1), dimensions={1,3,5}, to_apply=%region_0.1 | reduce | flops 57344 | bytes 294916 | tf_op jit(solution)/shard_map/reduce_sum | solution.py:95
  167.7 18.1 %reshape.79 = f32[8,2,16,2,64,2]{5,4,3,2,1,0:T(8,128)} reshape(f32[16,32,128]{2,1,0:T(8,128)S(1)} %fusion.5) | data formatting | bytes 524288 | tf_op jit(solution)/shard_map/reshape | solution.py:94
  185.8 7.0 %reduce_sum.155 = f32[8,16,64]{2,1,0:T(8,128)S(1)} reduce(f32[8,2,16,2,64,2]{5,4,3,2,1,0:T(8,128)} %reshape.79, f32[]{:T(128)} %constant.24.clone.1), dimensions={1,3,5}, to_apply=%region_4.5 | reduce | flops 57344 | bytes 294916 | tf_op jit(solution)/shard_map/reduce_sum | solution.py:95
  195.1 5.7 %collective-permute-start.30 = (f32[1,16,64]{2,1,0:T(8,128)S(1)}, f32[1,16,64]{2,1,0:T(8,128)S(1)}, u32[]{:S(2)}, u32[]{:S(2)}) collective-permute-start(f32[1,16,64]{2,1,0:T(8,128)S(1)} %get-tuple-element.63), channel_id=1, source_target_pairs={{0,32},{32,64},{64,96},{96,128},{128,160},{160,192},{192,224},{1,3... | collective-permute-start | bytes 12296 | tf_op jit(solution)/shard_map/ppermute | solution.py:22
  203.5 4.8 collective-permute-start.32
  210.5 4.3 collective-permute-start.34
  218.9 5.8 %collective-permute-start.36 = (f32[1,16,64]{2,1,0:T(8,128)S(1)}, f32[1,16,64]{2,1,0:T(8,128)S(1)}, u32[]{:S(2)}, u32[]{:S(2)}) collective-permute-start(f32[1,16,64]{2,1,0:T(8,128)S(1)} %get-tuple-element.61), channel_id=1, source_target_pairs={{0,32},{32,64},{64,96},{96,128},{128,160},{160,192},{192,224},{1,3... | collective-permute-start | bytes 12296 | tf_op jit(solution)/shard_map/ppermute | solution.py:22
  227.4 5.9 %collective-permute-start.38 = (f32[10,1,64]{2,1,0:T(1,128)S(1)}, f32[10,1,64]{2,1,0:T(1,128)S(1)}, u32[]{:S(2)}, u32[]{:S(2)}) collective-permute-start(f32[10,1,64]{2,1,0:T(1,128)S(1)} %get-tuple-element.51), channel_id=1, source_target_pairs={{0,4},{4,8},{8,12},{12,16},{16,20},{20,24},{24,28},{1,5},{5,9},{9,... | collective-permute-start | bytes 7688 | tf_op jit(solution)/shard_map/ppermute | solution.py:22
  235.5 4.7 collective-permute-start.40
  244.4 5.8 %collective-permute-start.42 = (f32[1,16,64]{2,1,0:T(8,128)S(1)}, f32[1,16,64]{2,1,0:T(8,128)S(1)}, u32[]{:S(2)}, u32[]{:S(2)}) collective-permute-start(f32[1,16,64]{2,1,0:T(8,128)S(1)} %get-tuple-element.59), channel_id=1, source_target_pairs={{0,32},{32,64},{64,96},{96,128},{128,160},{160,192},{192,224},{1,3... | collective-permute-start | bytes 12296 | tf_op jit(solution)/shard_map/ppermute | solution.py:22
  252.9 5.9 %collective-permute-start.44 = (f32[10,1,64]{2,1,0:T(1,128)S(1)}, f32[10,1,64]{2,1,0:T(1,128)S(1)}, u32[]{:S(2)}, u32[]{:S(2)}) collective-permute-start(f32[10,1,64]{2,1,0:T(1,128)S(1)} %get-tuple-element.49), channel_id=1, source_target_pairs={{0,4},{4,8},{8,12},{12,16},{16,20},{20,24},{24,28},{1,5},{5,9},{9,... | collective-permute-start | bytes 7688 | tf_op jit(solution)/shard_map/ppermute | solution.py:22
  261.0 4.7 collective-permute-start.46
  269.9 5.5 collective-permute-start.51
  279.1 5.3 collective-permute-start.53
  288.6 5.3 collective-permute-start.55
  302.7 6.4 %collective-permute-start.57 = (f32[1,8,32]{2,1,0:T(8,128)S(1)}, f32[1,8,32]{2,1,0:T(8,128)S(1)}, u32[]{:S(2)}, u32[]{:S(2)}) collective-permute-start(f32[1,8,32]{2,1,0:T(8,128)S(1)} %get-tuple-element.97), channel_id=1, source_target_pairs={{0,32},{32,64},{64,96},{96,128},{128,160},{160,192},{192,224},{1,3... | collective-permute-start | bytes 3080 | tf_op jit(solution)/shard_map/ppermute | solution.py:22
  309.9 4.8 collective-permute-start.59
  324.6 3.7 collective-permute-done.62
  329.8 5.7 %collective-permute-start.63 = (f32[1,8,32]{2,1,0:T(8,128)S(1)}, f32[1,8,32]{2,1,0:T(8,128)S(1)}, u32[]{:S(2)}, u32[]{:S(2)}) collective-permute-start(f32[1,8,32]{2,1,0:T(8,128)S(1)} %get-tuple-element.95), channel_id=1, source_target_pairs={{0,32},{32,64},{64,96},{96,128},{128,160},{160,192},{192,224},{1,3... | collective-permute-start | bytes 3080 | tf_op jit(solution)/shard_map/ppermute | solution.py:22
  336.3 4.2 collective-permute-start.65
  355.2 5.7 %collective-permute-start.69 = (f32[1,8,32]{2,1,0:T(8,128)S(1)}, f32[1,8,32]{2,1,0:T(8,128)S(1)}, u32[]{:S(2)}, u32[]{:S(2)}) collective-permute-start(f32[1,8,32]{2,1,0:T(8,128)S(1)} %get-tuple-element.93), channel_id=1, source_target_pairs={{0,32},{32,64},{64,96},{96,128},{128,160},{160,192},{192,224},{1,3... | collective-permute-start | bytes 3080 | tf_op jit(solution)/shard_map/ppermute | solution.py:22
  361.7 4.3 collective-permute-start.71
  372.4 4.0 collective-permute-start.73
  382.7 5.5 collective-permute-start.78
  408.9 6.4 %collective-permute-start.84 = (f32[1,4,16]{2,1,0:T(4,128)S(1)}, f32[1,4,16]{2,1,0:T(4,128)S(1)}, u32[]{:S(2)}, u32[]{:S(2)}) collective-permute-start(f32[1,4,16]{2,1,0:T(4,128)S(1)} %get-tuple-element.129), channel_id=1, source_target_pairs={{0,32},{32,64},{64,96},{96,128},{128,160},{160,192},{192,224},{1,3... | collective-permute-start | bytes 776 | tf_op jit(solution)/shard_map/ppermute | solution.py:22
  418.4 3.8 collective-permute-start.86
  430.8 5.7 %collective-permute-start.90 = (f32[1,4,16]{2,1,0:T(4,128)S(1)}, f32[1,4,16]{2,1,0:T(4,128)S(1)}, u32[]{:S(2)}, u32[]{:S(2)}) collective-permute-start(f32[1,4,16]{2,1,0:T(4,128)S(1)} %get-tuple-element.127), channel_id=1, source_target_pairs={{0,32},{32,64},{64,96},{96,128},{128,160},{160,192},{192,224},{1,3... | collective-permute-start | bytes 776 | tf_op jit(solution)/shard_map/ppermute | solution.py:22
  440.2 5.5 collective-permute-start.92
  454.4 5.7 %collective-permute-start.96 = (f32[1,4,16]{2,1,0:T(4,128)S(1)}, f32[1,4,16]{2,1,0:T(4,128)S(1)}, u32[]{:S(2)}, u32[]{:S(2)}) collective-permute-start(f32[1,4,16]{2,1,0:T(4,128)S(1)} %get-tuple-element.125), channel_id=1, source_target_pairs={{0,32},{32,64},{64,96},{96,128},{128,160},{160,192},{192,224},{1,3... | collective-permute-start | bytes 776 | tf_op jit(solution)/shard_map/ppermute | solution.py:22
  462.8 6.5 %collective-permute-start.98 = (f32[4,1,16]{2,1,0:T(1,128)S(1)}, f32[4,1,16]{2,1,0:T(1,128)S(1)}, u32[]{:S(2)}, u32[]{:S(2)}) collective-permute-start(f32[4,1,16]{2,1,0:T(1,128)S(1)} %get-tuple-element.117), channel_id=1, source_target_pairs={{0,4},{4,8},{8,12},{12,16},{16,20},{20,24},{24,28},{1,5},{5,9},{9,... | collective-permute-start | bytes 776 | tf_op jit(solution)/shard_map/ppermute | solution.py:22
  477.6 5.5 collective-permute-start.102
  485.8 6.5 %collective-permute-start.104 = (f32[4,1,16]{2,1,0:T(1,128)S(1)}, f32[4,1,16]{2,1,0:T(1,128)S(1)}, u32[]{:S(2)}, u32[]{:S(2)}) collective-permute-start(f32[4,1,16]{2,1,0:T(1,128)S(1)} %get-tuple-element.115), channel_id=1, source_target_pairs={{0,4},{4,8},{8,12},{12,16},{16,20},{20,24},{24,28},{1,5},{5,9},{9,... | collective-permute-start | bytes 776 | tf_op jit(solution)/shard_map/ppermute | solution.py:22
  499.5 67.2 %all-gather.1 = f32[256,2,8]{2,1,0:T(2,128)S(1)} all-gather(f32[1,2,8]{2,1,0:T(2,128)S(1)} %multiply_bitcast_fusion), channel_id=2, replica_groups=mesh['gx'=8,'gy'=8,'gz'=4] {'gx','gy','gz'}, dimensions={0}, use_global_device_ids=true | all-gather | bytes 16448 | tf_op jit(solution)/shard_map/all_gather | solution.py:207
  (388 shorter events, 218.1 us)
Async XLA Ops:
  1.4 17.6 %collective-permute-start = (f32[1,32,128]{2,1,0:T(8,128)S(1)}, f32[1,32,128]{2,1,0:T(8,128)S(1)}, u32[]{:S(2)}, u32[]{:S(2)}) collective-permute-start(f32[1,32,128]{2,1,0:T(8,128)S(1)} %slice.903), channel_id=1, source_target_pairs={{32,0},{64,32},{96,64},{128,96},{160,128},{192,160},{224,192},{33,... | collective-permute-start | bytes 49160 | tf_op jit(solution)/shard_map/ppermute | solution.py:34
  3.5 15.5 %collective-permute-start.1 = (f32[16,1,128]{2,1,0:T(1,128)S(1)}, f32[16,1,128]{2,1,0:T(1,128)S(1)}, u32[]{:S(2)}, u32[]{:S(2)}) collective-permute-start(f32[16,1,128]{2,1,0:T(1,128)S(1)} %slice.905), channel_id=1, source_target_pairs={{4,0},{8,4},{12,8},{16,12},{20,16},{24,20},{28,24},{5,1},{9,5},{13... | collective-permute-start | bytes 24584 | tf_op jit(solution)/shard_map/ppermute | solution.py:34
  8.7 10.2 %collective-permute-start.2 = (f32[16,32,1]{2,1,0:T(8,128)}, f32[16,32,1]{2,1,0:T(8,128)S(1)}, u32[]{:S(2)}, u32[]{:S(2)}) collective-permute-start(f32[16,32,1]{2,1,0:T(8,128)} %bitcast.27), channel_id=1, source_target_pairs={{1,0},{2,1},{3,2},{5,4},{6,5},{7,6},{9,8},{10,9},{11,10},{13,12},{... | collective-permute-start | bytes 6152 | tf_op jit(solution)/shard_map/ppermute | solution.py:34
  34.6 12.1 %collective-permute-start.8 = (f32[18,34,1]{2,1,0:T(8,128)S(1)}, f32[18,34,1]{2,1,0:T(8,128)S(1)}, u32[]{:S(2)}, u32[]{:S(2)}) collective-permute-start(f32[18,34,1]{2,1,0:T(8,128)S(1)} %get-tuple-element.22), channel_id=1, source_target_pairs={{1,0},{2,1},{3,2},{5,4},{6,5},{7,6},{9,8},{10,9},{11,10},{13,12},{... | collective-permute-start | bytes 7352 | tf_op jit(solution)/shard_map/ppermute | solution.py:24
  35.9 11.6 %collective-permute-start.7 = (f32[18,34,1]{2,1,0:T(8,128)S(1)}, f32[18,34,1]{2,1,0:T(8,128)S(1)}, u32[]{:S(2)}, u32[]{:S(2)}) collective-permute-start(f32[18,34,1]{2,1,0:T(8,128)S(1)} %get-tuple-element.21), channel_id=1, source_target_pairs={{0,1},{1,2},{2,3},{4,5},{5,6},{6,7},{8,9},{9,10},{10,11},{12,13},{... | collective-permute-start | bytes 7352 | tf_op jit(solution)/shard_map/ppermute | solution.py:22
  62.1 13.1 %collective-permute-start.14 = (f32[18,34,1]{2,1,0:T(8,128)S(1)}, f32[18,34,1]{2,1,0:T(8,128)S(1)}, u32[]{:S(2)}, u32[]{:S(2)}) collective-permute-start(f32[18,34,1]{2,1,0:T(8,128)S(1)} %get-tuple-element.20), channel_id=1, source_target_pairs={{1,0},{2,1},{3,2},{5,4},{6,5},{7,6},{9,8},{10,9},{11,10},{13,12},{... | collective-permute-start | bytes 7352 | tf_op jit(solution)/shard_map/ppermute | solution.py:24
  63.4 12.8 %collective-permute-start.13 = (f32[18,34,1]{2,1,0:T(8,128)S(1)}, f32[18,34,1]{2,1,0:T(8,128)S(1)}, u32[]{:S(2)}, u32[]{:S(2)}) collective-permute-start(f32[18,34,1]{2,1,0:T(8,128)S(1)} %get-tuple-element.19), channel_id=1, source_target_pairs={{0,1},{1,2},{2,3},{4,5},{5,6},{6,7},{8,9},{9,10},{10,11},{12,13},{... | collective-permute-start | bytes 7352 | tf_op jit(solution)/shard_map/ppermute | solution.py:22
  91.5 13.1 %collective-permute-start.20 = (f32[18,34,1]{2,1,0:T(8,128)}, f32[18,34,1]{2,1,0:T(8,128)S(1)}, u32[]{:S(2)}, u32[]{:S(2)}) collective-permute-start(f32[18,34,1]{2,1,0:T(8,128)} %get-tuple-element.18), channel_id=1, source_target_pairs={{1,0},{2,1},{3,2},{5,4},{6,5},{7,6},{9,8},{10,9},{11,10},{13,12},{... | collective-permute-start | bytes 7352 | tf_op jit(solution)/shard_map/ppermute | solution.py:24
  92.8 13.0 %collective-permute-start.19 = (f32[18,34,1]{2,1,0:T(8,128)S(1)}, f32[18,34,1]{2,1,0:T(8,128)S(1)}, u32[]{:S(2)}, u32[]{:S(2)}) collective-permute-start(f32[18,34,1]{2,1,0:T(8,128)S(1)} %get-tuple-element.17), channel_id=1, source_target_pairs={{0,1},{1,2},{2,3},{4,5},{5,6},{6,7},{8,9},{9,10},{10,11},{12,13},{... | collective-permute-start | bytes 7352 | tf_op jit(solution)/shard_map/ppermute | solution.py:22
  107.2 8.8 %collective-permute-start.25 = (f32[1,32,128]{2,1,0:T(8,128)S(1)}, f32[1,32,128]{2,1,0:T(8,128)S(1)}, u32[]{:S(2)}, u32[]{:S(2)}) collective-permute-start(f32[1,32,128]{2,1,0:T(8,128)S(1)} %get-tuple-element.32), channel_id=1, source_target_pairs={{32,0},{64,32},{96,64},{128,96},{160,128},{192,160},{224,192},{33,... | collective-permute-start | bytes 49160 | tf_op jit(solution)/shard_map/ppermute | solution.py:24
  108.5 7.5 %collective-permute-start.24 = (f32[1,32,128]{2,1,0:T(8,128)S(1)}, f32[1,32,128]{2,1,0:T(8,128)S(1)}, u32[]{:S(2)}, u32[]{:S(2)}) collective-permute-start(f32[1,32,128]{2,1,0:T(8,128)S(1)} %get-tuple-element.31), channel_id=1, source_target_pairs={{0,32},{32,64},{64,96},{96,128},{128,160},{160,192},{192,224},{1,3... | collective-permute-start | bytes 49160 | tf_op jit(solution)/shard_map/ppermute | solution.py:22
  113.3 79.4 %collective-permute-start.23 = (f32[8,16,1]{2,1,0:T(8,128)S(1)}, f32[8,16,1]{2,1,0:T(8,128)}, u32[]{:S(2)}, u32[]{:S(2)}) collective-permute-start(f32[8,16,1]{2,1,0:T(8,128)S(1)} %bitcast.30), channel_id=1, source_target_pairs={{1,0},{2,1},{3,2},{5,4},{6,5},{7,6},{9,8},{10,9},{11,10},{13,12},{... | collective-permute-start | bytes 1544 | tf_op jit(solution)/shard_map/ppermute | solution.py:34
  116.7 14.4 %collective-permute-start.27 = (f32[18,1,128]{2,1,0:T(1,128)}, f32[18,1,128]{2,1,0:T(1,128)}, u32[]{:S(2)}, u32[]{:S(2)}) collective-permute-start(f32[18,1,128]{2,1,0:T(1,128)} %get-tuple-element.24), channel_id=1, source_target_pairs={{4,0},{8,4},{12,8},{16,12},{20,16},{24,20},{28,24},{5,1},{9,5},{13... | collective-permute-start | bytes 27656 | tf_op jit(solution)/shard_map/ppermute | solution.py:24
  119.2 11.8 %collective-permute-start.26 = (f32[18,1,128]{2,1,0:T(1,128)}, f32[18,1,128]{2,1,0:T(1,128)}, u32[]{:S(2)}, u32[]{:S(2)}) collective-permute-start(f32[18,1,128]{2,1,0:T(1,128)} %get-tuple-element.23), channel_id=1, source_target_pairs={{0,4},{4,8},{8,12},{12,16},{16,20},{20,24},{24,28},{1,5},{5,9},{9,... | collective-permute-start | bytes 27656 | tf_op jit(solution)/shard_map/ppermute | solution.py:22
  122.9 69.9 %collective-permute-start.22 = (f32[8,1,64]{2,1,0:T(1,128)}, f32[8,1,64]{2,1,0:T(1,128)}, u32[]{:S(2)}, u32[]{:S(2)}) collective-permute-start(f32[8,1,64]{2,1,0:T(1,128)} %slice.1141), channel_id=1, source_target_pairs={{4,0},{8,4},{12,8},{16,12},{20,16},{24,20},{28,24},{5,1},{9,5},{13... | collective-permute-start | bytes 6152 | tf_op jit(solution)/shard_map/ppermute | solution.py:34
  133.0 33.3 %collective-permute-start.29 = (f32[18,34,1]{2,1,0:T(8,128)}, f32[18,34,1]{2,1,0:T(8,128)S(1)}, u32[]{:S(2)}, u32[]{:S(2)}) collective-permute-start(f32[18,34,1]{2,1,0:T(8,128)} %get-tuple-element.16), channel_id=1, source_target_pairs={{1,0},{2,1},{3,2},{5,4},{6,5},{7,6},{9,8},{10,9},{11,10},{13,12},{... | collective-permute-start | bytes 7352 | tf_op jit(solution)/shard_map/ppermute | solution.py:24
  134.2 32.1 %collective-permute-start.28 = (f32[18,34,1]{2,1,0:T(8,128)S(1)}, f32[18,34,1]{2,1,0:T(8,128)S(1)}, u32[]{:S(2)}, u32[]{:S(2)}) collective-permute-start(f32[18,34,1]{2,1,0:T(8,128)S(1)} %get-tuple-element.15), channel_id=1, source_target_pairs={{0,1},{1,2},{2,3},{4,5},{5,6},{6,7},{8,9},{9,10},{10,11},{12,13},{... | collective-permute-start | bytes 7352 | tf_op jit(solution)/shard_map/ppermute | solution.py:22
  139.6 53.2 %collective-permute-start.21 = (f32[1,16,64]{2,1,0:T(8,128)S(1)}, f32[1,16,64]{2,1,0:T(8,128)S(1)}, u32[]{:S(2)}, u32[]{:S(2)}) collective-permute-start(f32[1,16,64]{2,1,0:T(8,128)S(1)} %slice.1140), channel_id=1, source_target_pairs={{32,0},{64,32},{96,64},{128,96},{160,128},{192,160},{224,192},{33,... | collective-permute-start | bytes 12296 | tf_op jit(solution)/shard_map/ppermute | solution.py:34
  217.6 7.1 %collective-permute-start.37 = (f32[1,16,64]{2,1,0:T(8,128)S(1)}, f32[1,16,64]{2,1,0:T(8,128)S(1)}, u32[]{:S(2)}, u32[]{:S(2)}) collective-permute-start(f32[1,16,64]{2,1,0:T(8,128)S(1)} %get-tuple-element.62), channel_id=1, source_target_pairs={{32,0},{64,32},{96,64},{128,96},{160,128},{192,160},{224,192},{33,... | collective-permute-start | bytes 12296 | tf_op jit(solution)/shard_map/ppermute | solution.py:24
  225.5 7.9 %collective-permute-start.39 = (f32[10,1,64]{2,1,0:T(1,128)S(1)}, f32[10,1,64]{2,1,0:T(1,128)S(1)}, u32[]{:S(2)}, u32[]{:S(2)}) collective-permute-start(f32[10,1,64]{2,1,0:T(1,128)S(1)} %get-tuple-element.52), channel_id=1, source_target_pairs={{4,0},{8,4},{12,8},{16,12},{20,16},{24,20},{28,24},{5,1},{9,5},{13... | collective-permute-start | bytes 7688 | tf_op jit(solution)/shard_map/ppermute | solution.py:24
  243.1 7.1 %collective-permute-start.43 = (f32[1,16,64]{2,1,0:T(8,128)S(1)}, f32[1,16,64]{2,1,0:T(8,128)S(1)}, u32[]{:S(2)}, u32[]{:S(2)}) collective-permute-start(f32[1,16,64]{2,1,0:T(8,128)S(1)} %get-tuple-element.60), channel_id=1, source_target_pairs={{32,0},{64,32},{96,64},{128,96},{160,128},{192,160},{224,192},{33,... | collective-permute-start | bytes 12296 | tf_op jit(solution)/shard_map/ppermute | solution.py:24
  251.0 7.8 %collective-permute-start.45 = (f32[10,1,64]{2,1,0:T(1,128)S(1)}, f32[10,1,64]{2,1,0:T(1,128)S(1)}, u32[]{:S(2)}, u32[]{:S(2)}) collective-permute-start(f32[10,1,64]{2,1,0:T(1,128)S(1)} %get-tuple-element.50), channel_id=1, source_target_pairs={{4,0},{8,4},{12,8},{16,12},{20,16},{24,20},{28,24},{5,1},{9,5},{13... | collective-permute-start | bytes 7688 | tf_op jit(solution)/shard_map/ppermute | solution.py:24
  268.6 8.5 %collective-permute-start.52 = (f32[1,16,64]{2,1,0:T(8,128)S(1)}, f32[1,16,64]{2,1,0:T(8,128)S(1)}, u32[]{:S(2)}, u32[]{:S(2)}) collective-permute-start(f32[1,16,64]{2,1,0:T(8,128)S(1)} %get-tuple-element.58), channel_id=1, source_target_pairs={{32,0},{64,32},{96,64},{128,96},{160,128},{192,160},{224,192},{33,... | collective-permute-start | bytes 12296 | tf_op jit(solution)/shard_map/ppermute | solution.py:24
  269.9 7.2 %collective-permute-start.51 = (f32[1,16,64]{2,1,0:T(8,128)S(1)}, f32[1,16,64]{2,1,0:T(8,128)S(1)}, u32[]{:S(2)}, u32[]{:S(2)}) collective-permute-start(f32[1,16,64]{2,1,0:T(8,128)S(1)} %get-tuple-element.57), channel_id=1, source_target_pairs={{0,32},{32,64},{64,96},{96,128},{128,160},{160,192},{192,224},{1,3... | collective-permute-start | bytes 12296 | tf_op jit(solution)/shard_map/ppermute | solution.py:22
  275.4 25.9 %collective-permute-start.50 = (f32[4,8,1]{2,1,0:T(8,128)S(1)}, f32[4,8,1]{2,1,0:T(8,128)S(1)}, u32[]{:S(2)}, u32[]{:S(2)}) collective-permute-start(f32[4,8,1]{2,1,0:T(8,128)S(1)} %bitcast.35), channel_id=1, source_target_pairs={{1,0},{2,1},{3,2},{5,4},{6,5},{7,6},{9,8},{10,9},{11,10},{13,12},{... | collective-permute-start | bytes 392 | tf_op jit(solution)/shard_map/ppermute | solution.py:34
  277.1 10.0 %collective-permute-start.54 = (f32[10,1,64]{2,1,0:T(1,128)S(1)}, f32[10,1,64]{2,1,0:T(1,128)S(1)}, u32[]{:S(2)}, u32[]{:S(2)}) collective-permute-start(f32[10,1,64]{2,1,0:T(1,128)S(1)} %get-tuple-element.48), channel_id=1, source_target_pairs={{4,0},{8,4},{12,8},{16,12},{20,16},{24,20},{28,24},{5,1},{9,5},{13... | collective-permute-start | bytes 7688 | tf_op jit(solution)/shard_map/ppermute | solution.py:24
  279.1 8.1 %collective-permute-start.53 = (f32[10,1,64]{2,1,0:T(1,128)S(1)}, f32[10,1,64]{2,1,0:T(1,128)S(1)}, u32[]{:S(2)}, u32[]{:S(2)}) collective-permute-start(f32[10,1,64]{2,1,0:T(1,128)S(1)} %get-tuple-element.47), channel_id=1, source_target_pairs={{0,4},{4,8},{8,12},{12,16},{16,20},{20,24},{24,28},{1,5},{5,9},{9,... | collective-permute-start | bytes 7688 | tf_op jit(solution)/shard_map/ppermute | solution.py:22
  284.4 16.9 %collective-permute-start.49 = (f32[4,1,32]{2,1,0:T(1,128)S(1)}, f32[4,1,32]{2,1,0:T(1,128)S(1)}, u32[]{:S(2)}, u32[]{:S(2)}) collective-permute-start(f32[4,1,32]{2,1,0:T(1,128)S(1)} %slice.1160), channel_id=1, source_target_pairs={{4,0},{8,4},{12,8},{16,12},{20,16},{24,20},{28,24},{5,1},{9,5},{13... | collective-permute-start | bytes 1544 | tf_op jit(solution)/shard_map/ppermute | solution.py:34
  287.3 10.6 %collective-permute-start.56 = (f32[10,18,1]{2,1,0:T(8,128)S(1)}, f32[10,18,1]{2,1,0:T(8,128)S(1)}, u32[]{:S(2)}, u32[]{:S(2)}) collective-permute-start(f32[10,18,1]{2,1,0:T(8,128)S(1)} %get-tuple-element.40), channel_id=1, source_target_pairs={{1,0},{2,1},{3,2},{5,4},{6,5},{7,6},{9,8},{10,9},{11,10},{13,12},{... | collective-permute-start | bytes 2168 | tf_op jit(solution)/shard_map/ppermute | solution.py:24
  288.6 9.3 %collective-permute-start.55 = (f32[10,18,1]{2,1,0:T(8,128)S(1)}, f32[10,18,1]{2,1,0:T(8,128)S(1)}, u32[]{:S(2)}, u32[]{:S(2)}) collective-permute-start(f32[10,18,1]{2,1,0:T(8,128)S(1)} %get-tuple-element.39), channel_id=1, source_target_pairs={{0,1},{1,2},{2,3},{4,5},{5,6},{6,7},{8,9},{9,10},{10,11},{12,13},{... | collective-permute-start | bytes 2168 | tf_op jit(solution)/shard_map/ppermute | solution.py:22
  293.9 7.4 %collective-permute-start.48 = (f32[1,8,32]{2,1,0:T(8,128)S(1)}, f32[1,8,32]{2,1,0:T(8,128)S(1)}, u32[]{:S(2)}, u32[]{:S(2)}) collective-permute-start(f32[1,8,32]{2,1,0:T(8,128)S(1)} %slice.1159), channel_id=1, source_target_pairs={{32,0},{64,32},{96,64},{128,96},{160,128},{192,160},{224,192},{33,... | collective-permute-start | bytes 3080 | tf_op jit(solution)/shard_map/ppermute | solution.py:34
  301.4 7.7 %collective-permute-start.58 = (f32[1,8,32]{2,1,0:T(8,128)S(1)}, f32[1,8,32]{2,1,0:T(8,128)S(1)}, u32[]{:S(2)}, u32[]{:S(2)}) collective-permute-start(f32[1,8,32]{2,1,0:T(8,128)S(1)} %get-tuple-element.98), channel_id=1, source_target_pairs={{32,0},{64,32},{96,64},{128,96},{160,128},{192,160},{224,192},{33,... | collective-permute-start | bytes 3080 | tf_op jit(solution)/shard_map/ppermute | solution.py:24
  302.7 7.1 %collective-permute-start.57 = (f32[1,8,32]{2,1,0:T(8,128)S(1)}, f32[1,8,32]{2,1,0:T(8,128)S(1)}, u32[]{:S(2)}, u32[]{:S(2)}) collective-permute-start(f32[1,8,32]{2,1,0:T(8,128)S(1)} %get-tuple-element.97), channel_id=1, source_target_pairs={{0,32},{32,64},{64,96},{96,128},{128,160},{160,192},{192,224},{1,3... | collective-permute-start | bytes 3080 | tf_op jit(solution)/shard_map/ppermute | solution.py:22
  328.5 7.1 %collective-permute-start.64 = (f32[1,8,32]{2,1,0:T(8,128)S(1)}, f32[1,8,32]{2,1,0:T(8,128)S(1)}, u32[]{:S(2)}, u32[]{:S(2)}) collective-permute-start(f32[1,8,32]{2,1,0:T(8,128)S(1)} %get-tuple-element.96), channel_id=1, source_target_pairs={{32,0},{64,32},{96,64},{128,96},{160,128},{192,160},{224,192},{33,... | collective-permute-start | bytes 3080 | tf_op jit(solution)/shard_map/ppermute | solution.py:24
  353.9 7.2 %collective-permute-start.70 = (f32[1,8,32]{2,1,0:T(8,128)S(1)}, f32[1,8,32]{2,1,0:T(8,128)S(1)}, u32[]{:S(2)}, u32[]{:S(2)}) collective-permute-start(f32[1,8,32]{2,1,0:T(8,128)S(1)} %get-tuple-element.94), channel_id=1, source_target_pairs={{32,0},{64,32},{96,64},{128,96},{160,128},{192,160},{224,192},{33,... | collective-permute-start | bytes 3080 | tf_op jit(solution)/shard_map/ppermute | solution.py:24
  361.7 7.6 %collective-permute-start.71 = (f32[6,1,32]{2,1,0:T(1,128)S(1)}, f32[6,1,32]{2,1,0:T(1,128)S(1)}, u32[]{:S(2)}, u32[]{:S(2)}) collective-permute-start(f32[6,1,32]{2,1,0:T(1,128)S(1)} %get-tuple-element.83), channel_id=1, source_target_pairs={{0,4},{4,8},{8,12},{12,16},{16,20},{20,24},{24,28},{1,5},{5,9},{9,... | collective-permute-start | bytes 2312 | tf_op jit(solution)/shard_map/ppermute | solution.py:22
  366.0 41.5 %collective-permute-start.77 = (f32[2,4,1]{2,1,0:T(4,128)S(1)}, f32[2,4,1]{2,1,0:T(4,128)S(1)}, u32[]{:S(2)}, u32[]{:S(2)}) collective-permute-start(f32[2,4,1]{2,1,0:T(4,128)S(1)} %bitcast.38), channel_id=1, source_target_pairs={{1,0},{2,1},{3,2},{5,4},{6,5},{7,6},{9,8},{10,9},{11,10},{13,12},{... | collective-permute-start | bytes 104 | tf_op jit(solution)/shard_map/ppermute | solution.py:34
  381.4 9.0 %collective-permute-start.79 = (f32[1,8,32]{2,1,0:T(8,128)S(1)}, f32[1,8,32]{2,1,0:T(8,128)S(1)}, u32[]{:S(2)}, u32[]{:S(2)}) collective-permute-start(f32[1,8,32]{2,1,0:T(8,128)S(1)} %get-tuple-element.92), channel_id=1, source_target_pairs={{32,0},{64,32},{96,64},{128,96},{160,128},{192,160},{224,192},{33,... | collective-permute-start | bytes 3080 | tf_op jit(solution)/shard_map/ppermute | solution.py:24
  382.7 7.7 %collective-permute-start.78 = (f32[1,8,32]{2,1,0:T(8,128)S(1)}, f32[1,8,32]{2,1,0:T(8,128)S(1)}, u32[]{:S(2)}, u32[]{:S(2)}) collective-permute-start(f32[1,8,32]{2,1,0:T(8,128)S(1)} %get-tuple-element.91), channel_id=1, source_target_pairs={{0,32},{32,64},{64,96},{96,128},{128,160},{160,192},{192,224},{1,3... | collective-permute-start | bytes 3080 | tf_op jit(solution)/shard_map/ppermute | solution.py:22
  388.2 19.3 %collective-permute-start.76 = (f32[2,1,16]{2,1,0:T(1,128)S(1)}, f32[2,1,16]{2,1,0:T(1,128)S(1)}, u32[]{:S(2)}, u32[]{:S(2)}) collective-permute-start(f32[2,1,16]{2,1,0:T(1,128)S(1)} %slice.1185), channel_id=1, source_target_pairs={{4,0},{8,4},{12,8},{16,12},{20,16},{24,20},{28,24},{5,1},{9,5},{13... | collective-permute-start | bytes 392 | tf_op jit(solution)/shard_map/ppermute | solution.py:34
  394.1 13.5 %collective-permute-start.75 = (f32[1,4,16]{2,1,0:T(4,128)S(1)}, f32[1,4,16]{2,1,0:T(4,128)S(1)}, u32[]{:S(2)}, u32[]{:S(2)}) collective-permute-start(f32[1,4,16]{2,1,0:T(4,128)S(1)} %slice.1184), channel_id=1, source_target_pairs={{32,0},{64,32},{96,64},{128,96},{160,128},{192,160},{224,192},{33,... | collective-permute-start | bytes 776 | tf_op jit(solution)/shard_map/ppermute | solution.py:34
  407.6 7.7 %collective-permute-start.85 = (f32[1,4,16]{2,1,0:T(4,128)S(1)}, f32[1,4,16]{2,1,0:T(4,128)S(1)}, u32[]{:S(2)}, u32[]{:S(2)}) collective-permute-start(f32[1,4,16]{2,1,0:T(4,128)S(1)} %get-tuple-element.130), channel_id=1, source_target_pairs={{32,0},{64,32},{96,64},{128,96},{160,128},{192,160},{224,192},{33,... | collective-permute-start | bytes 776 | tf_op jit(solution)/shard_map/ppermute | solution.py:24
  408.9 7.1 %collective-permute-start.84 = (f32[1,4,16]{2,1,0:T(4,128)S(1)}, f32[1,4,16]{2,1,0:T(4,128)S(1)}, u32[]{:S(2)}, u32[]{:S(2)}) collective-permute-start(f32[1,4,16]{2,1,0:T(4,128)S(1)} %get-tuple-element.129), channel_id=1, source_target_pairs={{0,32},{32,64},{64,96},{96,128},{128,160},{160,192},{192,224},{1,3... | collective-permute-start | bytes 776 | tf_op jit(solution)/shard_map/ppermute | solution.py:22
  437.3 8.4 %collective-permute-start.93 = (f32[4,1,16]{2,1,0:T(1,128)S(1)}, f32[4,1,16]{2,1,0:T(1,128)S(1)}, u32[]{:S(2)}, u32[]{:S(2)}) collective-permute-start(f32[4,1,16]{2,1,0:T(1,128)S(1)} %get-tuple-element.120), channel_id=1, source_target_pairs={{4,0},{8,4},{12,8},{16,12},{20,16},{24,20},{28,24},{5,1},{9,5},{13... | collective-permute-start | bytes 776 | tf_op jit(solution)/shard_map/ppermute | solution.py:24
  460.8 8.4 %collective-permute-start.99 = (f32[4,1,16]{2,1,0:T(1,128)S(1)}, f32[4,1,16]{2,1,0:T(1,128)S(1)}, u32[]{:S(2)}, u32[]{:S(2)}) collective-permute-start(f32[4,1,16]{2,1,0:T(1,128)S(1)} %get-tuple-element.118), channel_id=1, source_target_pairs={{4,0},{8,4},{12,8},{16,12},{20,16},{24,20},{28,24},{5,1},{9,5},{13... | collective-permute-start | bytes 776 | tf_op jit(solution)/shard_map/ppermute | solution.py:24
  462.8 7.2 %collective-permute-start.98 = (f32[4,1,16]{2,1,0:T(1,128)S(1)}, f32[4,1,16]{2,1,0:T(1,128)S(1)}, u32[]{:S(2)}, u32[]{:S(2)}) collective-permute-start(f32[4,1,16]{2,1,0:T(1,128)S(1)} %get-tuple-element.117), channel_id=1, source_target_pairs={{0,4},{4,8},{8,12},{12,16},{16,20},{20,24},{24,28},{1,5},{5,9},{9,... | collective-permute-start | bytes 776 | tf_op jit(solution)/shard_map/ppermute | solution.py:22
  483.8 8.4 %collective-permute-start.105 = (f32[4,1,16]{2,1,0:T(1,128)S(1)}, f32[4,1,16]{2,1,0:T(1,128)S(1)}, u32[]{:S(2)}, u32[]{:S(2)}) collective-permute-start(f32[4,1,16]{2,1,0:T(1,128)S(1)} %get-tuple-element.116), channel_id=1, source_target_pairs={{4,0},{8,4},{12,8},{16,12},{20,16},{24,20},{28,24},{5,1},{9,5},{13... | collective-permute-start | bytes 776 | tf_op jit(solution)/shard_map/ppermute | solution.py:24
  485.8 7.2 %collective-permute-start.104 = (f32[4,1,16]{2,1,0:T(1,128)S(1)}, f32[4,1,16]{2,1,0:T(1,128)S(1)}, u32[]{:S(2)}, u32[]{:S(2)}) collective-permute-start(f32[4,1,16]{2,1,0:T(1,128)S(1)} %get-tuple-element.115), channel_id=1, source_target_pairs={{0,4},{4,8},{8,12},{12,16},{16,20},{20,24},{24,28},{1,5},{5,9},{9,... | collective-permute-start | bytes 776 | tf_op jit(solution)/shard_map/ppermute | solution.py:22
  (82 other events, 1144.6 us)
where the time goes:
time: 573 us; the launch traced here: 568 us
  starting transfers between devices  318 us (55%)
  waiting for transfers between devices  86 us (15%)
  blocking collectives  67.2 us (12%)
  local copies, waits for them, and re-layouts  59.1 us (10%)
  other arithmetic  34 us (6%)
    ppermute x48, starting transfers between devices, padded(): lax.ppermute(tail, axis, [(i, (i + 1) % count) for i in range(ends)])  218 us
    ppermute x48, starting transfers between devices, padded(): lax.ppermute(head, axis, [((i + 1) % count, i) for i in range(ends)])  79 us
    all_gather x1, blocking collectives, body(): lax.all_gather(source[None, None], ('gx', 'gy', 'gz'), axis=0, tiled=True)  67.2 us
    ppermute x48, waiting for transfers between devices, padded(): lax.ppermute(head, axis, [((i + 1) % count, i) for i in range(ends)])  52.9 us
    reshape x4, local copies, waits for them, and re-layouts, coarsen_cells(): field_values.reshape(span_x // 2, 2, span_y // 2, 2, span_z // 2, 2)  38.5 us
    ppermute x48, waiting for transfers between devices, padded(): lax.ppermute(tail, axis, [(i, (i + 1) % count) for i in range(ends)])  24.3 us
    ppermute x12, starting transfers between devices, shifted(): lax.ppermute(value, axis, [(source, source + steps) for source in range(i...  21.7 us
    reduce_sum x8, other arithmetic, coarsen_cells(): return jnp.mean(grouped, axis=(1, 3, 5))  14.9 us
  transfers between devices with their start and end apart: 108, of which 47 were waited for; matrix products, arithmetic and copies ran while one was open for 14% of the time, Pallas kernels for 0%

commit v1 on v0

v1 whole, which is shorter than its diff:
```python
import itertools

import jax
import jax.numpy as jnp
from jax import lax
from jax.experimental import pallas as pl
from jax.experimental.pallas import tpu as pltpu
from jax.sharding import PartitionSpec as P

MESH = pl.DeviceIdType.MESH
AXES = ("gx", "gy", "gz")
SIZES = (8, 8, 4)
SWEEPS = 4
F32 = jnp.float32

SIX = ((1, 0, 0), (-1, 0, 0), (0, 1, 0), (0, -1, 0), (0, 0, 1), (0, 0, -1))
BOX = tuple(d for d in itertools.product((-1, 0, 1), repeat=3) if d != (0, 0, 0))
COLUMNS = tuple(
    d for d in itertools.product((-1, 0, 1), (-1, 0, 1), range(4)) if d != (0, 0, 0)
)
PLANE = tuple(d for d in itertools.product(range(8), range(8), (0,)) if d != (0, 0, 0))

FIELDS = (
    ("a", "pair", "pair", "pair"),
    ("bx", "even", "pair", "pair"),
    ("by", "pair", "even", "pair"),
    ("bz", "pair", "pair", "even"),
    ("hx", "odd", "pair", "pair"),
    ("hy", "pair", "odd", "pair"),
    ("hz", "pair", "pair", "odd"),
)


def chebyshev_weights(count):
    middle, spread = 1.125, 0.875
    sharpness = middle / spread
    weights = [(0.0, 1.0 / middle)]
    rho_prev = 1.0 / sharpness
    for _ in range(1, count):
        rho_next = 1.0 / (2.0 * sharpness - rho_prev)
        weights.append((rho_next * rho_prev, 2.0 * rho_next / spread))
        rho_prev = rho_next
    return weights


WEIGHTS = chebyshev_weights(SWEEPS)


def neighbour(d):
    return tuple(
        lax.rem(lax.axis_index(a) + ((s + n) % n), n) for a, s, n in zip(AXES, d, SIZES)
    )


def iota(shape, dim):
    return lax.broadcasted_iota(jnp.int32, shape, dim)


def roll(value, shift, axis):
    n = value.shape[axis]
    if isinstance(shift, int):
        shift %= n
        if shift == 0:
            return value
    return pltpu.roll(value, shift, axis)


def picker(mode, first, count, out, scale):
    row = iota((128, 128), 0) - first
    col = iota((128, 128), 1) - out
    hit = (row >> 1) == col
    hit = hit & (col >= 0) & (col < count)
    if mode != "pair":
        hit = hit & ((row & 1) == (0 if mode == "even" else 1))
    return jnp.where(hit, scale, 0.0).astype(F32)


def dot(value, matrix):
    return jnp.dot(
        value, matrix, precision=lax.Precision.HIGHEST, preferred_element_type=F32
    )


def x_pick(value, mode):
    n = value.shape[0]
    grouped = value.reshape((n // 2, 2) + value.shape[1:])
    if mode == "pair":
        return grouped[:, 0] + grouped[:, 1]
    return grouped[:, 0 if mode == "even" else 1]


def y_pick(tmp, value, mode):
    rows = value.shape[0]
    tmp[0:rows, :] = value
    if mode == "pair":
        return tmp[pl.ds(0, rows // 2, stride=2), :] + tmp[pl.ds(1, rows // 2, stride=2), :]
    return tmp[pl.ds(0 if mode == "even" else 1, rows // 2, stride=2), :]


def kernel(
    src_h, a_h, bx_h, by_h, bz_h,
    o0_h, o1, o2, o3, o4,
    src, a0, bx, by, bz, hy, hz, diag, inv_s, gain, v,
    send_fx, send_fy, send_fz, next_x, next_y, next_z,
    recv_y, recv_z, send_y, send_z,
    tmp, fold,
    s1c, p1c, s1s, p1s, r1c, q1c, r1s, q1s, k1, u1,
    s2c, s2s, r2c, r2s, k2, u2,
    s3z, r3z, s3c, s3s, r3y, r3c, r3s, k3, u3, x3,
    in_sem, out_sem, send_sem, recv_sem,
):
    gx, gy, gz = (lax.axis_index(a) for a in AXES)
    used = [0]

    def push(source, target, d):
        k = used[0]
        used[0] += 1
        copy = pltpu.make_async_remote_copy(
            src_ref=source,
            dst_ref=target,
            send_sem=send_sem.at[k],
            recv_sem=recv_sem.at[k],
            device_id=neighbour(d),
            device_id_type=MESH,
        )
        copy.start()
        return copy

    def received(copies):
        for copy in copies:
            copy.wait_recv()

    def sent(copies):
        for copy in copies:
            copy.wait_send()

    barrier = pltpu.get_barrier_semaphore()
    for d in SIX:
        pl.semaphore_signal(barrier, inc=1, device_id=neighbour(d), device_id_type=MESH)

    loads = []
    for k, (h, m) in enumerate(
        ((bx_h, bx.at[0:16]), (by_h, by), (bz_h, bz), (a_h, a0), (src_h, src))
    ):
        copy = pltpu.make_async_copy(h, m, in_sem.at[k])
        copy.start()
        loads.append(copy)
    for copy in loads:
        copy.wait()

    lane = iota((8, 128), 1)
    sub = iota((8, 128), 0)
    lane32 = iota((32, 128), 1)
    inner_x = jnp.where(gx > 0, 1.0, 0.0).astype(F32)
    inner_y = jnp.where(gy > 0, 1.0, 0.0).astype(F32)
    inner_z = jnp.where(gz > 0, 1.0, 0.0).astype(F32)

    def pack_ends(packed, value, x):
        for j in range(4):
            at = 32 * j + 2 * x
            moved = roll(value[8 * j : 8 * j + 8, :], at + 1, 1)
            packed = moved if packed is None else jnp.where((lane >> 1) == (at >> 1), moved, packed)
        return packed

    def unpack_ends(ends, x):
        return jnp.concatenate([roll(ends, -(32 * j + 2 * x + 1), 1) for j in range(4)], axis=0)

    send_fx[...] = bx[0] * inner_x
    packed = None
    for x in range(16):
        send_fy[x : x + 1, :] = by[x, 0:1, :] * inner_y
        packed = pack_ends(packed, bz[x], x)
    send_fz[...] = packed * inner_z

    SHAPES = {1: (16, 32), 2: (8, 16), 3: (4, 8)}
    LANES = {1: (0, 64, 64), 2: (64, 32, 0), 3: (0, 16, 0)}
    OWN = {1: {}, 2: {}, 3: {}}

    def coarsen(level, names, fine):
        first, count, out = LANES[level]
        n, m = SHAPES[level]
        matrices = {}
        for k, (name, xm, ym, zm) in enumerate(FIELDS):
            if name not in names:
                continue
            if zm not in matrices:
                matrices[zm] = picker(zm, first, count, out, 1.0)
            value = x_pick(fine(name), xm).reshape(n // 2 * m, 128)
            value = dot(y_pick(tmp, value, ym), matrices[zm])
            OWN[level][k] = value * (0.125 if name == "a" else 0.25)

    INDEX = {f[0]: k for k, f in enumerate(FIELDS)}

    def own(level):
        n, m = SHAPES[level + 1] if level < 3 else (2, 4)
        return lambda name: OWN[level][INDEX[name]].reshape(n, m, 128)

    fine = {"a": a0, "by": by, "bz": bz, "hy": hy, "hz": hz}

    def level_zero(name):
        if name == "bx":
            return bx[0:16]
        if name == "hx":
            return bx[1:17]
        return fine[name][...]

    low = ("a", "bx", "by", "bz")
    high = ("hx", "hy", "hz")
    coarsen(1, low, level_zero)
    coarsen(2, low, own(1))
    coarsen(3, low, own(2))

    pl.semaphore_wait(barrier, 6)

    faces = [
        push(send_fx, next_x, (-1, 0, 0)),
        push(send_fy, next_y, (0, -1, 0)),
        push(send_fz, next_z, (0, 0, -1)),
    ]

    def swap_lanes(from_low, from_high):
        odd = (lane & 1) == 1
        return jnp.where(odd, roll(from_low, 1, 1), roll(from_high, -1, 1))

    def exchange(t):
        for x in range(16):
            send_y[t, 0, x : x + 1, :] = v[t, 1 + x, 8:9, :]
            send_y[t, 1, x : x + 1, :] = v[t, 1 + x, 39:40, :]
        return [
            push(v.at[t, 1, 8:40], v.at[t, 17, 8:40], (-1, 0, 0)),
            push(v.at[t, 16, 8:40], v.at[t, 0, 8:40], (1, 0, 0)),
            push(send_y.at[t, 0], recv_y.at[t, 1], (0, -1, 0)),
            push(send_y.at[t, 1], recv_y.at[t, 0], (0, 1, 0)),
            push(send_z.at[t], recv_z.at[t, 1], (0, 0, -1)),
            push(send_z.at[t], recv_z.at[t, 0], (0, 0, 1)),
        ]

    def land(t):
        for x in range(16):
            v[t, 1 + x, 7:8, :] = recv_y[t, 0, x : x + 1, :]
            v[t, 1 + x, 40:41, :] = recv_y[t, 1, x : x + 1, :]
        return swap_lanes(recv_z[t, 0], recv_z[t, 1])

    def around(t, x, ends):
        c = v[t, 1 + x, 8:40, :]
        halo = unpack_ends(ends, x)
        below = jnp.where(lane32 == 0, halo, roll(c, 1, 1))
        above = jnp.where(lane32 == 127, halo, roll(c, -1, 1))
        total = bx[x] * v[t, x, 8:40, :] + bx[x + 1] * v[t, x + 2, 8:40, :]
        total = total + (by[x] * v[t, 1 + x, 7:39, :] + hy[x] * v[t, 1 + x, 9:41, :])
        return c, total + (bz[x] * below + hz[x] * above)

    received(faces)
    bx[16] = next_x[...]
    ends = roll(next_z[...], -1, 1)
    packed = None
    row32 = iota((32, 128), 0)
    for x in range(16):
        b = by[x]
        up = jnp.where(row32 == 31, jnp.broadcast_to(next_y[x : x + 1, :], (32, 128)), roll(b, -1, 0))
        hy[x] = up
        total = (bx[x] + bx[x + 1]) + (b + up)
        b = bz[x]
        halo = jnp.concatenate([roll(ends, -(32 * j + 2 * x + 1), 1) for j in range(4)], axis=0)
        up = jnp.where(lane32 == 127, halo, roll(b, -1, 1))
        hz[x] = up
        total = a0[x] + (total + (b + up))
        diag[x] = total
        inverse = 1.0 / total
        inv_s[x] = inverse
        g = inverse * src[x]
        gain[x] = g
        g = g * WEIGHTS[0][1]
        v[0, 1 + x, 8:40, :] = g
        packed = pack_ends(packed, g, x)
    send_z[0] = packed
    rounds = [exchange(0)]

    coarsen(1, high, level_zero)
    coarsen(2, high, own(1))
    coarsen(3, high, own(2))
    bx[0] = bx[0] * inner_x
    for x in range(16):
        by[x, 0:1, :] = by[x, 0:1, :] * inner_y
        bz[x] = jnp.where(lane32 == 0, bz[x] * inner_z, bz[x])

    def own_coefficients(level):
        scale = 0.25**level
        get = OWN[level]
        a, lx, ly, lz, ux, uy, uz = (get[k] for k in range(7))
        d = a + scale * ((lx + ux) + (ly + uy) + (lz + uz))
        rows = d.shape[0]
        row = iota((rows, 128), 0)
        m = SHAPES[level][1] // 2
        first = LANES[level][2]
        lx = jnp.where(row < m, lx * inner_x, lx)
        ly = jnp.where((row & (m - 1)) == 0, ly * inner_y, ly)
        lz = jnp.where(iota((rows, 128), 1) == first, lz * inner_z, lz)
        return d, lx, ly, lz

    def pack_one(value):
        lane16 = iota((16, 128), 1) >> 2
        packed = None
        for x in range(8):
            moved = roll(value[16 * x : 16 * x + 16, :], 4 * x + 4, 1)
            if packed is None:
                packed = moved
            else:
                packed = jnp.where((lane16 == x) | (lane16 == x + 17), moved, packed)
        return packed

    def send_one(s, p, r, q):
        copies = []
        for d in BOX:
            dx, dy, dz = d
            xs = {0: pl.ds(0, 8), 1: pl.ds(4, 4), -1: pl.ds(0, 4)}[dx]
            xd = {0: pl.ds(4, 8), 1: pl.ds(0, 4), -1: pl.ds(12, 4)}[dx]
            ys = {0: pl.ds(0, 16), 1: pl.ds(8, 8), -1: pl.ds(0, 8)}[dy]
            yd = {0: pl.ds(0, 16), 1: pl.ds(24, 8), -1: pl.ds(16, 8)}[dy]
            if dz == 0:
                copies.append(push(s.at[:, xs, ys], r.at[:, xd, yd], d))
            else:
                copies.append(push(p.at[:, ys], q.at[:, 0 if dz == 1 else 1, 1 - dx, yd], d))
        return copies

    def ring_rows(value):
        halo = jnp.where(sub < 4, value[16:24, :], value[24:32, :])
        return jnp.concatenate([value[0:16, :], halo], axis=0)

    def assemble_one(r, q, f, out):
        lane24 = iota((24, 128), 1)
        for b, (start, rows) in enumerate(((0, range(4, 8)), (4, range(8)), (12, range(4)))):
            m = ring_rows(jnp.where(lane32 < 64, q[f, 0, b], q[f, 1, b]))
            for n, xl in enumerate(rows):
                c = ring_rows(r[f, start + n])
                out[start + n] = jnp.where(lane24 >= 64, c, roll(m, 60 - 4 * xl, 1))

    fields = own_coefficients(1)
    for f, value in enumerate(fields):
        value3 = value.reshape(8, 16, 128)
        s1c[f] = value3
        r1c[f, 4:12, 0:16, :] = value3
        p1c[f] = pack_one(value)

    def pack_two(value):
        packed = value[0:8, :]
        for x in range(1, 4):
            packed = packed + roll(value[8 * x : 8 * x + 8, :], 32 * x, 1)
        return packed

    def send_two(s, r):
        return [push(s, r.at[1 - d[0], 1 - d[1], gz], d) for d in COLUMNS]

    def assemble_two(get, out):
        for b in range(3):
            for t in range(2):
                tiles = []
                for z in range(4):
                    if t == 0:
                        tiles.append(get(b, 1, z))
                    else:
                        tiles.append(jnp.where(sub < 4, get(b, 2, z), get(b, 0, z)))
                for x in range(4):
                    value = roll(tiles[0], -32 * x, 1)
                    for z in range(1, 4):
                        value = jnp.where((lane >> 5) == z, roll(tiles[z], 32 * (z - x), 1), value)
                    out[4 * b + x, 8 * t : 8 * t + 8, :] = value

    def sweep(t):
        momentum, step = WEIGHTS[t + 1]
        ends = land(t)
        packed = None
        for x in range(16):
            c, total = around(t, x, ends)
            new = (1.0 + momentum - step) * c + step * (gain[x] + inv_s[x] * total)
            if t > 0:
                new = new - momentum * v[t - 1, 1 + x, 8:40, :]
            v[t + 1, 1 + x, 8:40, :] = new
            packed = pack_ends(packed, new, x)
        send_z[t + 1] = packed
        rounds.append(exchange(t + 1))

    sent(faces)
    received(rounds[0])
    sweep(0)

    for f, value in enumerate(own_coefficients(2)):
        s2c[f] = pack_two(value)
    r2c[1, 1, gz] = s2c[...]
    for f, value in enumerate(own_coefficients(3)):
        halves = jnp.where(sub < 4, value, roll(value, 64, 1))
        halves = halves + roll(halves, 4, 0)
        s3z[f] = roll(halves, 16 * gz, 1)[0:4, :]
    r3z[gz] = s3z[...]
    three_columns = [push(s3z, r3z.at[gz], (0, 0, d)) for d in (1, 2, 3)]

    sent(rounds[0])
    received(rounds[1])
    sweep(1)

    one_coefficients = send_one(s1c, p1c, r1c, q1c)
    received(three_columns)
    s3c[...] = (r3z[0] + r3z[1]) + (r3z[2] + r3z[3])
    r3y[gy] = s3c[...]
    sent(three_columns)

    def prepare(k, planes, scale):
        for x in range(planes):
            d = k[0, x]
            inverse = 1.0 / jnp.where(d > 0, d, 1.0)
            k[4, x] = inverse
            k[5, x] = scale * inverse
            k[6, x] = roll(k[2, x], -1, 0)
            k[7, x] = roll(k[3, x], -1, 1)

    sent(rounds[1])
    received(rounds[2])
    sweep(2)

    result = pltpu.make_async_copy(v.at[3, 1:17, 8:40], o0_h, out_sem)
    result.start()

    two_coefficients = send_two(s2c, r2c)
    three_rows = [push(s3c, r3y.at[gy], (0, d, 0)) for d in range(1, 8)]
    received(one_coefficients)
    for f in range(4):
        assemble_one(r1c, q1c, f, k1.at[f])
    prepare(k1, 16, 0.25)
    sent(one_coefficients)
    sent(rounds[2])
    received(rounds[3])

    ends = land(3)
    for x in range(0, 16, 2):
        pair = None
        for y in (x, x + 1):
            c, total = around(3, y, ends)
            r = (src[y] - diag[y] * c) + total
            pair = r if pair is None else pair + r
        fold[16 * x : 16 * x + 32, :] = pair
    value = fold[pl.ds(0, 128, stride=2), :] + fold[pl.ds(1, 128, stride=2), :]
    value = dot(value, picker("pair", 0, 64, 64, 0.125))
    s1s[0] = value.reshape(8, 16, 128)
    r1s[0, 4:12, 0:16, :] = s1s[0]
    p1s[0] = pack_one(value)
    one_source = send_one(s1s, p1s, r1s, q1s)

    received(three_rows)
    r3c[gx] = r3y[...]
    three_coefficients = [push(r3y, r3c.at[gx], (d, 0, 0)) for d in range(1, 8)]
    received(two_coefficients)
    for f in range(4):
        assemble_two(lambda b, y, z, f=f: r2c[b, y, z, f], k2.at[f])
    prepare(k2, 12, 0.25**2)
    sent(two_coefficients)
    sent(three_rows)
    sent(rounds[3])
    received(one_source)

    def wide_around(k, c, lower, upper, x):
        total = k[1, x] * lower + k[1, x + 1] * upper
        total = total + (k[2, x] * roll(c, 1, 0) + k[6, x] * roll(c, -1, 0))
        return total + (k[3, x] * roll(c, 1, 1) + k[7, x] * roll(c, -1, 1))

    def wide_level(k, u, planes):
        for x in range(planes):
            g = k[4, x] * k[8, x]
            k[9, x] = g
            u[0, x] = WEIGHTS[0][1] * g
        for t in range(1, SWEEPS):
            momentum, step = WEIGHTS[t]
            for x in range(t, planes - t):
                c = u[t - 1, x]
                total = wide_around(k, c, u[t - 1, x - 1], u[t - 1, x + 1], x)
                new = (1.0 + momentum - step) * c + step * (k[9, x] + k[5, x] * total)
                if t > 1:
                    new = new - momentum * u[t - 2, x]
                u[t, x] = new

    def wide_residual(k, u, x, scale):
        c = u[3, x]
        total = wide_around(k, c, u[3, x - 1], u[3, x + 1], x)
        return (k[8, x] - k[0, x] * c) + scale * total

    assemble_one(r1s, q1s, 0, k1.at[8])
    wide_level(k1, u1, 16)
    lane16 = iota((16, 128), 1)
    for x in range(4):
        r = wide_residual(k1, u1, 4 + 2 * x, 0.25) + wide_residual(k1, u1, 5 + 2 * x, 0.25)
        fold[16 * x : 16 * x + 16, :] = jnp.where(lane16 >= 64, r[0:16, :], 0.0)
    value = fold[pl.ds(0, 32, stride=2), :] + fold[pl.ds(1, 32, stride=2), :]
    value = dot(value, picker("pair", 64, 32, 0, 0.125))
    s2s[...] = pack_two(value)
    r2s[1, 1, gz] = s2s[...]
    two_source = send_two(s2s, r2s)
    for x in range(8):
        o1[x] = roll(u1[3, 4 + x, 0:16, :], 64, 1)[:, 0:64]
    received(three_coefficients)
    for y in range(8):
        for f in range(4):
            k3[f, :, 4 * y : 4 * y + 4, :] = r3c[:, y, f]
    lane8 = iota((32, 128), 1)
    for x in range(8):
        inverse = 1.0 / k3[0, x]
        k3[4, x] = inverse
        k3[5, x] = 0.25**3 * inverse
        k3[6, x] = roll(k3[2, x], -1, 0)
        k3[7, x] = roll(k3[3, x], -1, 1)
        here, after = roll(k3[1, x], 64, 1), roll(k3[1, (x + 1) % 8], 64, 1)
        k3[10, x] = jnp.where(lane8 < 64, here, after)
    sent(one_source)
    sent(three_coefficients)
    received(two_source)

    assemble_two(lambda b, y, z: r2s[b, y, z], k2.at[8])
    wide_level(k2, u2, 12)
    for x in range(2):
        r = wide_residual(k2, u2, 4 + 2 * x, 0.25**2) + wide_residual(k2, u2, 5 + 2 * x, 0.25**2)
        fold[8 * x : 8 * x + 8, :] = r[0:8, :]
    value = fold[pl.ds(0, 8, stride=2), :] + fold[pl.ds(1, 8, stride=2), :]
    value = dot(value, picker("pair", 0, 64, 0, 0.125))
    halves = jnp.where(sub < 4, value, roll(value, 64, 1))
    s3s[...] = (halves + roll(halves, 4, 0))[0:4, :]
    r3s[gx, gy] = s3s[...]
    three_source = [push(s3s, r3s.at[gx, gy], d) for d in PLANE]
    for x in range(4):
        o2[x] = roll(u2[3, 4 + x, 0:8, :], 128 - 32 * gz, 1)[:, 0:32]
    sent(two_source)
    received(three_source)

    for y in range(8):
        k3[8, :, 4 * y : 4 * y + 4, :] = r3s[:, y]

    def whole_around(t, x):
        c = u3[t, x]
        turned = roll(c, 64, 1)
        lower = jnp.where(lane8 < 64, roll(u3[t, (x + 7) % 8], 64, 1), turned)
        upper = jnp.where(lane8 < 64, turned, roll(u3[t, (x + 1) % 8], 64, 1))
        total = k3[1, x] * lower + k3[10, x] * upper
        total = total + (k3[2, x] * roll(c, 1, 0) + k3[6, x] * roll(c, -1, 0))
        return c, total + (k3[3, x] * roll(c, 1, 1) + k3[7, x] * roll(c, -1, 1))

    for x in range(8):
        g = k3[4, x] * k3[8, x]
        k3[9, x] = g
        u3[0, x] = WEIGHTS[0][1] * g
    for t in range(1, SWEEPS):
        momentum, step = WEIGHTS[t]
        for x in range(8):
            c, total = whole_around(t - 1, x)
            new = (1.0 + momentum - step) * c + step * (k3[9, x] + k3[5, x] * total)
            if t > 1:
                new = new - momentum * u3[t - 2, x]
            u3[t, x] = new
    for x in range(8):
        c, total = whole_around(3, x)
        r = (k3[8, x] - k3[0, x] * c) + 0.25**3 * total
        fold[32 * x : 32 * x + 32, :] = r + roll(r, 64, 1)
        for y in range(8):
            x3[x, y, 0:4, :] = c[4 * y : 4 * y + 4, :]
    value = fold[pl.ds(0, 128, stride=2), :] + fold[pl.ds(1, 128, stride=2), :]
    value = dot(value, picker("pair", 0, 32, 0, 0.125))
    o4[...] = value.reshape(8, 16, 128)[:, :, 0:32]
    mine = x3[gx, gy]
    for half in range(2):
        o3[half] = roll(mine, (128 - 64 * half) - 16 * gz, 1)[0:4, 0:16]
    sent(three_source)
    result.wait()


def body(*args):
    vm = lambda *shape: pltpu.VMEM(shape, F32)
    scratch = [
        vm(16, 32, 128), vm(16, 32, 128), vm(17, 32, 128), vm(16, 32, 128), vm(16, 32, 128),
        vm(16, 32, 128), vm(16, 32, 128), vm(16, 32, 128), vm(16, 32, 128), vm(16, 32, 128),
        vm(4, 18, 48, 128),
        vm(32, 128), vm(16, 128), vm(8, 128), vm(32, 128), vm(16, 128), vm(8, 128),
        vm(4, 2, 16, 128), vm(4, 2, 8, 128), vm(4, 2, 16, 128), vm(4, 8, 128),
        vm(256, 128), vm(256, 128),
        vm(4, 8, 16, 128), vm(4, 16, 128), vm(1, 8, 16, 128), vm(1, 16, 128),
        vm(4, 16, 32, 128), vm(4, 2, 3, 32, 128), vm(1, 16, 32, 128), vm(1, 2, 3, 32, 128),
        vm(10, 16, 24, 128), vm(4, 16, 24, 128),
        vm(4, 8, 128), vm(8, 128), vm(3, 3, 4, 4, 8, 128), vm(3, 3, 4, 8, 128),
        vm(10, 12, 16, 128), vm(4, 12, 16, 128),
        vm(4, 4, 128), vm(4, 4, 4, 128), vm(4, 4, 128), vm(4, 128),
        vm(8, 4, 4, 128), vm(8, 8, 4, 4, 128), vm(8, 8, 4, 128), vm(11, 8, 32, 128), vm(4, 8, 32, 128),
        vm(8, 8, 8, 128),
        pltpu.SemaphoreType.DMA((5,)), pltpu.SemaphoreType.DMA,
        pltpu.SemaphoreType.DMA((288,)), pltpu.SemaphoreType.DMA((288,)),
    ]
    out = lambda *shape: jax.ShapeDtypeStruct(shape, F32)
    return pl.pallas_call(
        kernel,
        out_shape=(out(16, 32, 128), out(8, 16, 64), out(4, 8, 32), out(2, 4, 16), out(8, 16, 32)),
        in_specs=[pl.BlockSpec(memory_space=pl.ANY)] * 5,
        out_specs=[pl.BlockSpec(memory_space=pl.ANY)] + [pl.BlockSpec(memory_space=pltpu.VMEM)] * 4,
        scratch_shapes=scratch,
        compiler_params=pltpu.CompilerParams(
            collective_id=0, has_side_effects=True, vmem_limit_bytes=48 * 2**20
        ),
    )(*args)


def solution(mesh):
    spec = P(*AXES)
    return jax.shard_map(
        body,
        mesh=mesh,
        in_specs=(spec,) * 5,
        out_specs=(spec, spec, spec, spec, P()),
        check_vma=False,
    )
```

time: 573 us -> 73.9 us (0.13)
  starting transfers between devices: 318 us -> 0 us
  waiting for transfers between devices: 86 us -> 0 us
  blocking collectives: 67.2 us -> 0 us
  Pallas kernels: 0 us -> 65.1 us
  local copies, waits for them, and re-layouts: 59.1 us -> 7.9 us
  other arithmetic: 34 us -> 0 us
    ppermute x108 -> x0, starting transfers between devices: 318 us -> none  [the longest x48 218 us: padded(): lax.ppermute(tail, axis, [(i, (i + 1) % count) for i in range(ends)])]
    ppermute x108 -> x0, waiting for transfers between devices: 86 us -> none  [the longest x48 52.9 us: padded(): lax.ppermute(head, axis, [((i + 1) % count, i) for i in range(ends)])]
    all_gather x1 -> x0, blocking collectives: 67.2 us -> none  [body(): lax.all_gather(source[None, None], ('gx', 'gy', 'gz'), axis=0, tiled=True)]
    pallas_call x0 -> x1, Pallas kernels: none -> 65.1 us  [body(): pl.pallas_call(kernel, out_shape=(out(16, 32, 128), out(8, 16, 64), out(4...]
    reshape x5 -> x0, local copies, waits for them, and re-layouts: 38.6 us -> none  [the longest x4 38.5 us: coarsen_cells(): field_values.reshape(span_x // 2, 2, span_y // 2, 2, span_z // 2, 2)]
    reduce_sum x17 -> x0, other arithmetic: 19.6 us -> none  [the longest x8 14.9 us: coarsen_cells(): return jnp.mean(grouped, axis=(1, 3, 5))]
    slice x62 -> x0, local copies, waits for them, and re-layouts: 15.5 us -> none  [the longest x3 7.06 us: coarsen_faces(): even_faces = face_values[:, :, 0::2]]
    unnamed x52 -> x15, local copies, waits for them, and re-layouts: 0.16 us -> 7.9 us
  transfers between devices with their start and end apart: 108 -> 0, of which waited for: 47 -> 0; matrix products, arithmetic and copies ran while one was open for 14% -> 0% of each run, Pallas kernels for 0% -> 0%
where the time goes in v1:
time: 73.9 us; the launch traced here: 73.7 us
  Pallas kernels  65.1 us (88%)
  local copies, waits for them, and re-layouts  7.9 us (11%)
    pallas_call x1, Pallas kernels, body(): pl.pallas_call(kernel, out_shape=(out(16, 32, 128), out(8, 16, 64), out(4...  65.1 us
    unnamed x15, local copies, waits for them, and re-layouts  7.9 us

profile of v1, /device:TPU:1, one launch (start us, length us, event | category | flops | bytes accessed | tf_op | source)
XLA Modules:
  0.0 73.7 jit_solution(15567637180943904924)
XLA Ops:
  0.6 0.0 copy-start
  0.6 0.9 %copy-done = f32[16,32,128]{2,1,0:T(8,128)S(1)} copy-done((f32[16,32,128]{2,1,0:T(8,128)S(1)}, f32[16,32,128]{2,1,0:T(8,128)}, u32[]{:S(2)}) %copy-start) | copy-done | bytes 262168
  1.6 0.0 copy-start.1
  1.6 0.9 %copy-done.1 = f32[16,32,128]{2,1,0:T(8,128)S(1)} copy-done((f32[16,32,128]{2,1,0:T(8,128)S(1)}, f32[16,32,128]{2,1,0:T(8,128)}, u32[]{:S(2)}) %copy-start.1) | copy-done | bytes 262168
  2.5 0.0 copy-start.2
  2.5 0.9 %copy-done.2 = f32[16,32,128]{2,1,0:T(8,128)S(1)} copy-done((f32[16,32,128]{2,1,0:T(8,128)S(1)}, f32[16,32,128]{2,1,0:T(8,128)}, u32[]{:S(2)}) %copy-start.2) | copy-done | bytes 262168
  3.5 0.0 copy-start.3
  3.5 0.9 %copy-done.3 = f32[16,32,128]{2,1,0:T(8,128)S(1)} copy-done((f32[16,32,128]{2,1,0:T(8,128)S(1)}, f32[16,32,128]{2,1,0:T(8,128)}, u32[]{:S(2)}) %copy-start.3) | copy-done | bytes 262168
  4.4 0.0 copy-start.4
  4.4 0.9 %copy-done.4 = f32[16,32,128]{2,1,0:T(8,128)S(1)} copy-done((f32[16,32,128]{2,1,0:T(8,128)S(1)}, f32[16,32,128]{2,1,0:T(8,128)}, u32[]{:S(2)}) %copy-start.4) | copy-done | bytes 262168
  5.4 65.1 %shard_map.92 = (f32[16,32,128]{2,1,0:T(8,128)S(1)}, f32[8,16,64]{2,1,0:T(8,128)S(1)}, f32[4,8,32]{2,1,0:T(8,128)S(1)}, f32[2,4,16]{2,1,0:T(4,128)S(1)}, f32[8,16,32]{2,1,0:T(8,128)S(1)}) custom-call(f32[16,32,128]{2,1,0:T(8,128)S(1)} %copy-done, f32[16,32,128]{2,1,0:T(8,128)S(1)} %copy-done.1, f32[16,32,128]{2,1,0:T(8,128)S(1)} %copy-done.2, ...), custom_call_target="tpu_custom_call" | custom-call | tf_op jit(solution)/shard_map/pallas_call | solution.py:592
  70.5 0.7 copy.15
  71.2 0.6 copy.16
  71.9 0.6 copy.17
  72.5 0.6 copy.18
  73.1 0.6 copy.19
Async XLA Ops:
  0.6 1.0 %copy-start = (f32[16,32,128]{2,1,0:T(8,128)S(1)}, f32[16,32,128]{2,1,0:T(8,128)}, u32[]{:S(2)}) copy-start(f32[16,32,128]{2,1,0:T(8,128)} %src_h.1) | copy-start | bytes 786436
  1.6 0.9 %copy-start.1 = (f32[16,32,128]{2,1,0:T(8,128)S(1)}, f32[16,32,128]{2,1,0:T(8,128)}, u32[]{:S(2)}) copy-start(f32[16,32,128]{2,1,0:T(8,128)} %a_h.1) | copy-start | bytes 786436
  2.5 0.9 %copy-start.2 = (f32[16,32,128]{2,1,0:T(8,128)S(1)}, f32[16,32,128]{2,1,0:T(8,128)}, u32[]{:S(2)}) copy-start(f32[16,32,128]{2,1,0:T(8,128)} %bx_h.1) | copy-start | bytes 786436
  3.5 0.9 %copy-start.3 = (f32[16,32,128]{2,1,0:T(8,128)S(1)}, f32[16,32,128]{2,1,0:T(8,128)}, u32[]{:S(2)}) copy-start(f32[16,32,128]{2,1,0:T(8,128)} %by_h.1) | copy-start | bytes 786436
  4.4 0.9 %copy-start.4 = (f32[16,32,128]{2,1,0:T(8,128)S(1)}, f32[16,32,128]{2,1,0:T(8,128)}, u32[]{:S(2)}) copy-start(f32[16,32,128]{2,1,0:T(8,128)} %bz_h.1) | copy-start | bytes 786436

commit v2 on v1

--- a/solution.py
+++ b/solution.py
@@ -13,12 +13,20 @@
 SWEEPS = 4
 F32 = jnp.float32
 
-SIX = ((1, 0, 0), (-1, 0, 0), (0, 1, 0), (0, -1, 0), (0, 0, 1), (0, 0, -1))
-BOX = tuple(d for d in itertools.product((-1, 0, 1), repeat=3) if d != (0, 0, 0))
-COLUMNS = tuple(
-    d for d in itertools.product((-1, 0, 1), (-1, 0, 1), range(4)) if d != (0, 0, 0)
-)
-PLANE = tuple(d for d in itertools.product(range(8), range(8), (0,)) if d != (0, 0, 0))
+
+def distance(d):
+    return sum(min(s % n, -s % n) for s, n in zip(d, SIZES))
+
+
+def farthest_first(xs, ys, zs):
+    directions = [d for d in itertools.product(xs, ys, zs) if d != (0, 0, 0)]
+    return tuple(sorted(directions, key=lambda d: -distance(d)))
+
+
+BOX = farthest_first((-1, 0, 1), (-1, 0, 1), (-1, 0, 1))
+COLUMNS = farthest_first((-1, 0, 1), (-1, 0, 1), (0, 1, 2, 3))
+PLANE = farthest_first(range(8), range(8), (0,))
+SIX = tuple(d for d in BOX if distance(d) == 1)
 
 FIELDS = (
     ("a", "pair", "pair", "pair"),
@@ -106,13 +114,13 @@
     tmp, fold,
     s1c, p1c, s1s, p1s, r1c, q1c, r1s, q1s, k1, u1,
     s2c, s2s, r2c, r2s, k2, u2,
-    s3z, r3z, s3c, s3s, r3y, r3c, r3s, k3, u3, x3,
+    r3, s3s, r3s, k3, u3, x3,
     in_sem, out_sem, send_sem, recv_sem,
 ):
     gx, gy, gz = (lax.axis_index(a) for a in AXES)
     used = [0]
 
-    def push(source, target, d):
+    def push(source, target, d, device=None):
         k = used[0]
         used[0] += 1
         copy = pltpu.make_async_remote_copy(
@@ -120,7 +128,7 @@
             dst_ref=target,
             send_sem=send_sem.at[k],
             recv_sem=recv_sem.at[k],
-            device_id=neighbour(d),
+            device_id=neighbour(d) if device is None else device,
             device_id_type=MESH,
         )
         copy.start()
@@ -206,9 +214,6 @@
 
     low = ("a", "bx", "by", "bz")
     high = ("hx", "hy", "hz")
-    coarsen(1, low, level_zero)
-    coarsen(2, low, own(1))
-    coarsen(3, low, own(2))
 
     pl.semaphore_wait(barrier, 6)
 
@@ -222,17 +227,23 @@
         odd = (lane & 1) == 1
         return jnp.where(odd, roll(from_low, 1, 1), roll(from_high, -1, 1))
 
-    def exchange(t):
+    ORDER = (0, 15) + tuple(range(1, 15))
+
+    def exchange_x(t):
+        return [
+            push(v.at[t, 1, 8:40], v.at[t, 17, 8:40], (-1, 0, 0)),
+            push(v.at[t, 16, 8:40], v.at[t, 0, 8:40], (1, 0, 0)),
+        ]
+
+    def exchange_yz(t):
         for x in range(16):
             send_y[t, 0, x : x + 1, :] = v[t, 1 + x, 8:9, :]
             send_y[t, 1, x : x + 1, :] = v[t, 1 + x, 39:40, :]
         return [
-            push(v.at[t, 1, 8:40], v.at[t, 17, 8:40], (-1, 0, 0)),
-            push(v.at[t, 16, 8:40], v.at[t, 0, 8:40], (1, 0, 0)),
+            push(send_z.at[t], recv_z.at[t, 1], (0, 0, -1)),
+            push(send_z.at[t], recv_z.at[t, 0], (0, 0, 1)),
             push(send_y.at[t, 0], recv_y.at[t, 1], (0, -1, 0)),
             push(send_y.at[t, 1], recv_y.at[t, 0], (0, 1, 0)),
-            push(send_z.at[t], recv_z.at[t, 1], (0, 0, -1)),
-            push(send_z.at[t], recv_z.at[t, 0], (0, 0, 1)),
         ]
 
     def land(t):
@@ -255,7 +266,7 @@
     ends = roll(next_z[...], -1, 1)
     packed = None
     row32 = iota((32, 128), 0)
-    for x in range(16):
+    for x in ORDER:
         b = by[x]
         up = jnp.where(row32 == 31, jnp.broadcast_to(next_y[x : x + 1, :], (32, 128)), roll(b, -1, 0))
         hy[x] = up
@@ -273,9 +284,14 @@
         g = g * WEIGHTS[0][1]
         v[0, 1 + x, 8:40, :] = g
         packed = pack_ends(packed, g, x)
+        if x == 15:
+            rounds = [exchange_x(0)]
     send_z[0] = packed
-    rounds = [exchange(0)]
-
+    rounds[0] += exchange_yz(0)
+
+    coarsen(1, low, level_zero)
+    coarsen(2, low, own(1))
+    coarsen(3, low, own(2))
     coarsen(1, high, level_zero)
     coarsen(2, high, own(1))
     coarsen(3, high, own(2))
@@ -309,38 +325,38 @@
                 packed = jnp.where((lane16 == x) | (lane16 == x + 17), moved, packed)
         return packed
 
-    def send_one(s, p, r, q):
+    def send_one(s, p, r, q, reach):
         copies = []
         for d in BOX:
+            if distance(d) not in reach:
+                continue
             dx, dy, dz = d
             xs = {0: pl.ds(0, 8), 1: pl.ds(4, 4), -1: pl.ds(0, 4)}[dx]
             xd = {0: pl.ds(4, 8), 1: pl.ds(0, 4), -1: pl.ds(12, 4)}[dx]
-            ys = {0: pl.ds(0, 16), 1: pl.ds(8, 8), -1: pl.ds(0, 8)}[dy]
-            yd = {0: pl.ds(0, 16), 1: pl.ds(24, 8), -1: pl.ds(16, 8)}[dy]
+            ys = {0: pl.ds(0, 16), 1: pl.ds(12, 4), -1: pl.ds(0, 4)}[dy]
+            yd = {0: pl.ds(0, 16), 1: pl.ds(20, 4), -1: pl.ds(16, 4)}[dy]
             if dz == 0:
                 copies.append(push(s.at[:, xs, ys], r.at[:, xd, yd], d))
             else:
                 copies.append(push(p.at[:, ys], q.at[:, 0 if dz == 1 else 1, 1 - dx, yd], d))
         return copies
 
-    def ring_rows(value):
-        halo = jnp.where(sub < 4, value[16:24, :], value[24:32, :])
-        return jnp.concatenate([value[0:16, :], halo], axis=0)
-
-    def assemble_one(r, q, f, out):
-        lane24 = iota((24, 128), 1)
+    lane24 = iota((24, 128), 1)
+
+    def assemble_one(get, q, f, out):
         for b, (start, rows) in enumerate(((0, range(4, 8)), (4, range(8)), (12, range(4)))):
-            m = ring_rows(jnp.where(lane32 < 64, q[f, 0, b], q[f, 1, b]))
+            m = jnp.where(lane24 < 64, q[f, 0, b], q[f, 1, b])
             for n, xl in enumerate(rows):
-                c = ring_rows(r[f, start + n])
-                out[start + n] = jnp.where(lane24 >= 64, c, roll(m, 60 - 4 * xl, 1))
+                out[start + n] = jnp.where(lane24 >= 64, get(start + n), roll(m, 60 - 4 * xl, 1))
 
     fields = own_coefficients(1)
     for f, value in enumerate(fields):
-        value3 = value.reshape(8, 16, 128)
-        s1c[f] = value3
-        r1c[f, 4:12, 0:16, :] = value3
         p1c[f] = pack_one(value)
+    for f in range(2):
+        value = (fields[2 * f] + roll(fields[2 * f + 1], 64, 1)).reshape(8, 16, 128)
+        s1c[f] = value
+        r1c[f, 4:12, 0:16, :] = value
+    one_coefficients = send_one(s1c, p1c, r1c, q1c, (1,))
 
     def pack_two(value):
         packed = value[0:8, :]
@@ -348,18 +364,23 @@
             packed = packed + roll(value[8 * x : 8 * x + 8, :], 32 * x, 1)
         return packed
 
-    def send_two(s, r):
-        return [push(s, r.at[1 - d[0], 1 - d[1], gz], d) for d in COLUMNS]
+    def send_two(s, r, reach):
+        copies = []
+        for d in COLUMNS:
+            if distance(d) not in reach:
+                continue
+            target = r.at[1 - d[0], 1 if d[1] else 0, gz]
+            if d[1] == 0:
+                copies.append(push(s, target, d))
+            else:
+                half = pl.ds(4, 4) if d[1] == 1 else pl.ds(0, 4)
+                copies.append(push(s.at[:, half], target.at[:, half], d))
+        return copies
 
     def assemble_two(get, out):
         for b in range(3):
             for t in range(2):
-                tiles = []
-                for z in range(4):
-                    if t == 0:
-                        tiles.append(get(b, 1, z))
-                    else:
-                        tiles.append(jnp.where(sub < 4, get(b, 2, z), get(b, 0, z)))
+                tiles = [get(b, t, z) for z in range(4)]
                 for x in range(4):
                     value = roll(tiles[0], -32 * x, 1)
                     for z in range(1, 4):
@@ -370,39 +391,40 @@
         momentum, step = WEIGHTS[t + 1]
         ends = land(t)
         packed = None
-        for x in range(16):
+        for x in ORDER:
             c, total = around(t, x, ends)
             new = (1.0 + momentum - step) * c + step * (gain[x] + inv_s[x] * total)
             if t > 0:
                 new = new - momentum * v[t - 1, 1 + x, 8:40, :]
             v[t + 1, 1 + x, 8:40, :] = new
             packed = pack_ends(packed, new, x)
+            if x == 15:
+                rounds.append(exchange_x(t + 1))
         send_z[t + 1] = packed
-        rounds.append(exchange(t + 1))
+        rounds[t + 1] += exchange_yz(t + 1)
 
     sent(faces)
     received(rounds[0])
     sweep(0)
 
+    one_coefficients += send_one(s1c, p1c, r1c, q1c, (2,))
     for f, value in enumerate(own_coefficients(2)):
         s2c[f] = pack_two(value)
-    r2c[1, 1, gz] = s2c[...]
+    r2c[1, 0, gz] = s2c[...]
+    halves_of = lambda value: jnp.where(sub < 4, value, roll(value, 64, 1))
+    total = None
     for f, value in enumerate(own_coefficients(3)):
-        halves = jnp.where(sub < 4, value, roll(value, 64, 1))
-        halves = halves + roll(halves, 4, 0)
-        s3z[f] = roll(halves, 16 * gz, 1)[0:4, :]
-    r3z[gz] = s3z[...]
-    three_columns = [push(s3z, r3z.at[gz], (0, 0, d)) for d in (1, 2, 3)]
+        halves = halves_of(value)
+        halves = roll(halves + roll(halves, 4, 0), 16 * f, 1)
+        total = halves if total is None else total + halves
+    parity, chip = gy % 2, gy // 2
+    r3[parity, chip, gz, gx] = total[0:4, :]
 
     sent(rounds[0])
     received(rounds[1])
     sweep(1)
-
-    one_coefficients = send_one(s1c, p1c, r1c, q1c)
-    received(three_columns)
-    s3c[...] = (r3z[0] + r3z[1]) + (r3z[2] + r3z[3])
-    r3y[gy] = s3c[...]
-    sent(three_columns)
+    one_coefficients += send_one(s1c, p1c, r1c, q1c, (3,))
+    two_coefficients = send_two(s2c, r2c, (1, 2, 3))
 
     def prepare(k, planes, scale):
         for x in range(planes):
@@ -416,15 +438,19 @@
     sent(rounds[1])
     received(rounds[2])
     sweep(2)
+    two_coefficients += send_two(s2c, r2c, (4,))
+    block = r3.at[parity, chip, gz, gx]
+    three_x = [push(block, block, (d, 0, 0)) for d in (4, 3, 5, 2, 6, 1, 7)]
 
     result = pltpu.make_async_copy(v.at[3, 1:17, 8:40], o0_h, out_sem)
     result.start()
 
-    two_coefficients = send_two(s2c, r2c)
-    three_rows = [push(s3c, r3y.at[gy], (0, d, 0)) for d in range(1, 8)]
     received(one_coefficients)
     for f in range(4):
-        assemble_one(r1c, q1c, f, k1.at[f])
+        if f % 2 == 0:
+            assemble_one(lambda x, f=f: r1c[f // 2, x], q1c, f, k1.at[f])
+        else:
+            assemble_one(lambda x, f=f: roll(r1c[f // 2, x], 64, 1), q1c, f, k1.at[f])
     prepare(k1, 16, 0.25)
     sent(one_coefficients)
     sent(rounds[2])
@@ -443,17 +469,20 @@
     s1s[0] = value.reshape(8, 16, 128)
     r1s[0, 4:12, 0:16, :] = s1s[0]
     p1s[0] = pack_one(value)
-    one_source = send_one(s1s, p1s, r1s, q1s)
-
-    received(three_rows)
-    r3c[gx] = r3y[...]
-    three_coefficients = [push(r3y, r3c.at[gx], (d, 0, 0)) for d in range(1, 8)]
+    one_source = send_one(s1s, p1s, r1s, q1s, (1, 2, 3))
+
+    received(three_x)
+    block = r3.at[parity, chip, gz]
+    three_z = [push(block, block, (0, 0, d)) for d in (2, 1, 3)]
     received(two_coefficients)
     for f in range(4):
-        assemble_two(lambda b, y, z, f=f: r2c[b, y, z, f], k2.at[f])
+        assemble_two(lambda b, t, z, f=f: r2c[b, t, z, f], k2.at[f])
     prepare(k2, 12, 0.25**2)
     sent(two_coefficients)
-    sent(three_rows)
+    sent(three_x)
+    received(three_z)
+    block = r3.at[parity, chip]
+    three_y = [push(block, block, (0, d, 0)) for d in (4, 2, 6)]
     sent(rounds[3])
     received(one_source)
 
@@ -482,7 +511,7 @@
         total = wide_around(k, c, u[3, x - 1], u[3, x + 1], x)
         return (k[8, x] - k[0, x] * c) + scale * total
 
-    assemble_one(r1s, q1s, 0, k1.at[8])
+    assemble_one(lambda x: r1s[0, x], q1s, 0, k1.at[8])
     wide_level(k1, u1, 16)
     lane16 = iota((16, 128), 1)
     for x in range(4):
@@ -490,15 +519,25 @@
         fold[16 * x : 16 * x + 16, :] = jnp.where(lane16 >= 64, r[0:16, :], 0.0)
     value = fold[pl.ds(0, 32, stride=2), :] + fold[pl.ds(1, 32, stride=2), :]
     value = dot(value, picker("pair", 64, 32, 0, 0.125))
-    s2s[...] = pack_two(value)
-    r2s[1, 1, gz] = s2s[...]
-    two_source = send_two(s2s, r2s)
+    s2s[0] = pack_two(value)
+    r2s[1, 0, gz] = s2s[...]
+    two_source = send_two(s2s, r2s, (1, 2, 3, 4))
+    sent(three_z)
+    received(three_y)
+    block = r3.at[parity]
+    three_core = [push(block, block, None, (gx, gy + 1 - 2 * parity, gz))]
     for x in range(8):
         o1[x] = roll(u1[3, 4 + x, 0:16, :], 64, 1)[:, 0:64]
-    received(three_coefficients)
-    for y in range(8):
-        for f in range(4):
-            k3[f, :, 4 * y : 4 * y + 4, :] = r3c[:, y, f]
+    received(three_core)
+    group = (lane >> 4) & 3
+    for x in range(8):
+        for p in range(4):
+            tiles = [jnp.concatenate([r3[0, p, z, x], r3[1, p, z, x]], axis=0) for z in range(4)]
+            for f in range(4):
+                value = roll(tiles[0], -16 * f, 1)
+                for z in range(1, 4):
+                    value = jnp.where(group == z, roll(tiles[z], 16 * (z - f), 1), value)
+                k3[f, x, 8 * p : 8 * p + 8, :] = value
     lane8 = iota((32, 128), 1)
     for x in range(8):
         inverse = 1.0 / k3[0, x]
@@ -509,23 +548,24 @@
         here, after = roll(k3[1, x], 64, 1), roll(k3[1, (x + 1) % 8], 64, 1)
         k3[10, x] = jnp.where(lane8 < 64, here, after)
     sent(one_source)
-    sent(three_coefficients)
+    sent(three_y)
     received(two_source)
 
-    assemble_two(lambda b, y, z: r2s[b, y, z], k2.at[8])
+    assemble_two(lambda b, t, z: r2s[b, t, z, 0], k2.at[8])
     wide_level(k2, u2, 12)
     for x in range(2):
         r = wide_residual(k2, u2, 4 + 2 * x, 0.25**2) + wide_residual(k2, u2, 5 + 2 * x, 0.25**2)
         fold[8 * x : 8 * x + 8, :] = r[0:8, :]
     value = fold[pl.ds(0, 8, stride=2), :] + fold[pl.ds(1, 8, stride=2), :]
     value = dot(value, picker("pair", 0, 64, 0, 0.125))
-    halves = jnp.where(sub < 4, value, roll(value, 64, 1))
+    halves = halves_of(value)
     s3s[...] = (halves + roll(halves, 4, 0))[0:4, :]
     r3s[gx, gy] = s3s[...]
     three_source = [push(s3s, r3s.at[gx, gy], d) for d in PLANE]
     for x in range(4):
         o2[x] = roll(u2[3, 4 + x, 0:8, :], 128 - 32 * gz, 1)[:, 0:32]
     sent(two_source)
+    sent(three_core)
     received(three_source)
 
     for y in range(8):
@@ -568,6 +608,11 @@
     result.wait()
 
 
+def hand_over(*refs):
+    for k in range(5):
+        refs[5 + k][...] = refs[k][...]
+
+
 def body(*args):
     vm = lambda *shape: pltpu.VMEM(shape, F32)
     scratch = [
@@ -577,28 +622,33 @@
         vm(32, 128), vm(16, 128), vm(8, 128), vm(32, 128), vm(16, 128), vm(8, 128),
         vm(4, 2, 16, 128), vm(4, 2, 8, 128), vm(4, 2, 16, 128), vm(4, 8, 128),
         vm(256, 128), vm(256, 128),
-        vm(4, 8, 16, 128), vm(4, 16, 128), vm(1, 8, 16, 128), vm(1, 16, 128),
-        vm(4, 16, 32, 128), vm(4, 2, 3, 32, 128), vm(1, 16, 32, 128), vm(1, 2, 3, 32, 128),
+        vm(2, 8, 16, 128), vm(4, 16, 128), vm(1, 8, 16, 128), vm(1, 16, 128),
+        vm(2, 16, 24, 128), vm(4, 2, 3, 24, 128), vm(1, 16, 24, 128), vm(1, 2, 3, 24, 128),
         vm(10, 16, 24, 128), vm(4, 16, 24, 128),
-        vm(4, 8, 128), vm(8, 128), vm(3, 3, 4, 4, 8, 128), vm(3, 3, 4, 8, 128),
+        vm(4, 8, 128), vm(1, 8, 128), vm(3, 2, 4, 4, 8, 128), vm(3, 2, 4, 1, 8, 128),
         vm(10, 12, 16, 128), vm(4, 12, 16, 128),
-        vm(4, 4, 128), vm(4, 4, 4, 128), vm(4, 4, 128), vm(4, 128),
-        vm(8, 4, 4, 128), vm(8, 8, 4, 4, 128), vm(8, 8, 4, 128), vm(11, 8, 32, 128), vm(4, 8, 32, 128),
+        vm(2, 4, 4, 8, 4, 128), vm(4, 128), vm(8, 8, 4, 128), vm(11, 8, 32, 128), vm(4, 8, 32, 128),
         vm(8, 8, 8, 128),
         pltpu.SemaphoreType.DMA((5,)), pltpu.SemaphoreType.DMA,
         pltpu.SemaphoreType.DMA((288,)), pltpu.SemaphoreType.DMA((288,)),
     ]
     out = lambda *shape: jax.ShapeDtypeStruct(shape, F32)
-    return pl.pallas_call(
+    results = pl.pallas_call(
         kernel,
         out_shape=(out(16, 32, 128), out(8, 16, 64), out(4, 8, 32), out(2, 4, 16), out(8, 16, 32)),
         in_specs=[pl.BlockSpec(memory_space=pl.ANY)] * 5,
         out_specs=[pl.BlockSpec(memory_space=pl.ANY)] + [pl.BlockSpec(memory_space=pltpu.VMEM)] * 4,
         scratch_shapes=scratch,
         compiler_params=pltpu.CompilerParams(
-            collective_id=0, has_side_effects=True, vmem_limit_bytes=48 * 2**20
+            collective_id=0, has_side_effects=True, vmem_limit_bytes=63 * 2**20
         ),
     )(*args)
+    return pl.pallas_call(
+        hand_over,
+        out_shape=tuple(out(*r.shape) for r in results),
+        in_specs=[pl.BlockSpec(memory_space=pltpu.VMEM)] * 5,
+        out_specs=[pl.BlockSpec(memory_space=pltpu.VMEM)] * 5,
+    )(*results)
 
 
 def solution(mesh):

time: 73.9 us -> 56.3 us (0.76)
  Pallas kernels: 65.1 us -> 55.5 us
  local copies, waits for them, and re-layouts: 7.9 us -> 0 us
    pallas_call x1, Pallas kernels: 65.1 us -> 53.8 us  [body(): pl.pallas_call(kernel, out_shape=(out(16, 32, 128), out(8, 16, 64), out(4...]
    unnamed x15 -> x0, local copies, waits for them, and re-layouts: 7.9 us -> none
    pallas_call x0 -> x1, Pallas kernels: none -> 1.75 us  [body(): pl.pallas_call(hand_over, out_shape=tuple((out(*r.shape) for r in results...]
where the time goes in v2:
time: 56.3 us; the launch traced here: 56.2 us
  Pallas kernels  55.5 us (99%)
  between operations  0.64 us (1%)
    pallas_call x1, Pallas kernels, body(): pl.pallas_call(kernel, out_shape=(out(16, 32, 128), out(8, 16, 64), out(4...  53.8 us
    pallas_call x1, Pallas kernels, body(): pl.pallas_call(hand_over, out_shape=tuple((out(*r.shape) for r in results...  1.75 us

profile of v2, /device:TPU:1, one launch (start us, length us, event | category | flops | bytes accessed | tf_op | source)
XLA Modules:
  0.0 56.2 jit_solution(9181641908420062563)
XLA Ops:
  0.6 53.8 %shard_map.92 = (f32[16,32,128]{2,1,0:T(8,128)}, f32[8,16,64]{2,1,0:T(8,128)}, f32[4,8,32]{2,1,0:T(8,128)}, f32[2,4,16]{2,1,0:T(4,128)}, f32[8,16,32]{2,1,0:T(8,128)}) custom-call(f32[16,32,128]{2,1,0:T(8,128)} %src_h.1, f32[16,32,128]{2,1,0:T(8,128)} %a_h.1, f32[16,32,128]{2,1,0:T(8,128)} %bx_h.1, f32[16,32,128]{2,1,0:T(8,128)} %by_h.1, f32[16,32,128]{2,1,0:T(8,128)} %bz_h.1), custom_call_target="tpu_custom_call" | custom-call | tf_op jit(solution)/shard_map/pallas_call | solution.py:636
  54.4 1.8 %shard_map.93 = (f32[16,32,128]{2,1,0:T(8,128)}, f32[8,16,64]{2,1,0:T(8,128)}, f32[4,8,32]{2,1,0:T(8,128)}, f32[2,4,16]{2,1,0:T(4,128)}, f32[8,16,32]{2,1,0:T(8,128)}) custom-call(f32[16,32,128]{2,1,0:T(8,128)} %get-tuple-element.10.refs_0_, f32[8,16,64]{2,1,0:T(8,128)} %get-tuple-element.11.refs_1_, f32[4,8,32]{2,1,0:T(8,128)} %get-tuple-element.12.refs_2_, ...), custom_call_target="tpu_custom_call" | custom-call | tf_op jit(solution)/shard_map/pallas_call | solution.py:646

commit v3 on v2

--- a/solution.py
+++ b/solution.py
@@ -27,6 +27,9 @@
 COLUMNS = farthest_first((-1, 0, 1), (-1, 0, 1), (0, 1, 2, 3))
 PLANE = farthest_first(range(8), range(8), (0,))
 SIX = tuple(d for d in BOX if distance(d) == 1)
+
+FACES, ROUND, ONE_C, ONE_S, TWO_C, TWO_S = 0, 1, 5, 6, 7, 8
+THREE_X, THREE_Z, THREE_Y, THREE_CORE, THREE_S, GROUPS = 9, 10, 11, 12, 13, 14
 
 FIELDS = (
     ("a", "pair", "pair", "pair"),
@@ -73,20 +76,23 @@
     return pltpu.roll(value, shift, axis)
 
 
-def picker(mode, first, count, out, scale):
+def picker(mode, first, count, out):
     row = iota((128, 128), 0) - first
     col = iota((128, 128), 1) - out
     hit = (row >> 1) == col
     hit = hit & (col >= 0) & (col < count)
     if mode != "pair":
         hit = hit & ((row & 1) == (0 if mode == "even" else 1))
-    return jnp.where(hit, scale, 0.0).astype(F32)
+    return jnp.where(hit, 1.0, 0.0).astype(jnp.bfloat16)
 
 
 def dot(value, matrix):
-    return jnp.dot(
-        value, matrix, precision=lax.Precision.HIGHEST, preferred_element_type=F32
-    )
+    high = value.astype(jnp.bfloat16)
+    rest = value - high.astype(F32)
+    middle = rest.astype(jnp.bfloat16)
+    low = (rest - middle.astype(F32)).astype(jnp.bfloat16)
+    parts = jnp.concatenate([high, middle, low], axis=1)
+    return jnp.dot(parts, jnp.concatenate([matrix] * 3, axis=0), preferred_element_type=F32)
 
 
 def x_pick(value, mode):
@@ -114,33 +120,35 @@
     tmp, fold,
     s1c, p1c, s1s, p1s, r1c, q1c, r1s, q1s, k1, u1,
     s2c, s2s, r2c, r2s, k2, u2,
-    r3, s3s, r3s, k3, u3, x3,
+    r3, s3s, r3s, k3, u3, x3, gauge,
     in_sem, out_sem, send_sem, recv_sem,
 ):
     gx, gy, gz = (lax.axis_index(a) for a in AXES)
-    used = [0]
-
-    def push(source, target, d, device=None):
-        k = used[0]
-        used[0] += 1
-        copy = pltpu.make_async_remote_copy(
+    rows = {}
+
+    def push(group, source, target, d, device=None):
+        n = 1
+        for extent in target.shape[:-1]:
+            n *= extent
+        rows[group] = rows.get(group, 0) + n
+        pltpu.make_async_remote_copy(
             src_ref=source,
             dst_ref=target,
-            send_sem=send_sem.at[k],
-            recv_sem=recv_sem.at[k],
+            send_sem=send_sem.at[group],
+            recv_sem=recv_sem.at[group],
             device_id=neighbour(d) if device is None else device,
             device_id_type=MESH,
-        )
-        copy.start()
-        return copy
-
-    def received(copies):
-        for copy in copies:
-            copy.wait_recv()
-
-    def sent(copies):
-        for copy in copies:
-            copy.wait_send()
+        ).start()
+
+    def wait(group, sem):
+        measure = gauge.at[0 : rows[group]]
+        pltpu.make_async_copy(measure, measure, sem.at[group]).wait()
+
+    def received(group):
+        wait(group, recv_sem)
+
+    def sent(group):
+        wait(group, send_sem)
 
     barrier = pltpu.get_barrier_semaphore()
     for d in SIX:
@@ -187,15 +195,21 @@
     def coarsen(level, names, fine):
         first, count, out = LANES[level]
         n, m = SHAPES[level]
-        matrices = {}
+        size = n * m // 4
+        groups = {"pair": [], "even": []}
         for k, (name, xm, ym, zm) in enumerate(FIELDS):
             if name not in names:
                 continue
-            if zm not in matrices:
-                matrices[zm] = picker(zm, first, count, out, 1.0)
-            value = x_pick(fine(name), xm).reshape(n // 2 * m, 128)
-            value = dot(y_pick(tmp, value, ym), matrices[zm])
-            OWN[level][k] = value * (0.125 if name == "a" else 0.25)
+            value = y_pick(tmp, x_pick(fine(name), xm).reshape(n // 2 * m, 128), ym)
+            if zm == "odd":
+                value = roll(value, -1, 1)
+            groups["pair" if zm == "pair" else "even"].append((k, name, value))
+        for zm, members in groups.items():
+            value = jnp.concatenate([part for _, _, part in members], axis=0)
+            value = dot(value, picker(zm, first, count, out))
+            for at, (k, name, _) in enumerate(members):
+                part = value[at * size : (at + 1) * size, :]
+                OWN[level][k] = part * (0.125 if name == "a" else 0.25)
 
     INDEX = {f[0]: k for k, f in enumerate(FIELDS)}
 
@@ -215,13 +229,15 @@
     low = ("a", "bx", "by", "bz")
     high = ("hx", "hy", "hz")
 
+    coarsen(1, low, level_zero)
+    coarsen(2, low, own(1))
+    coarsen(3, low, own(2))
+
     pl.semaphore_wait(barrier, 6)
 
-    faces = [
-        push(send_fx, next_x, (-1, 0, 0)),
-        push(send_fy, next_y, (0, -1, 0)),
-        push(send_fz, next_z, (0, 0, -1)),
-    ]
+    push(FACES, send_fx, next_x, (-1, 0, 0))
+    push(FACES, send_fy, next_y, (0, -1, 0))
+    push(FACES, send_fz, next_z, (0, 0, -1))
 
     def swap_lanes(from_low, from_high):
         odd = (lane & 1) == 1
@@ -230,21 +246,17 @@
     ORDER = (0, 15) + tuple(range(1, 15))
 
     def exchange_x(t):
-        return [
-            push(v.at[t, 1, 8:40], v.at[t, 17, 8:40], (-1, 0, 0)),
-            push(v.at[t, 16, 8:40], v.at[t, 0, 8:40], (1, 0, 0)),
-        ]
+        push(ROUND + t, v.at[t, 1, 8:40], v.at[t, 17, 8:40], (-1, 0, 0))
+        push(ROUND + t, v.at[t, 16, 8:40], v.at[t, 0, 8:40], (1, 0, 0))
 
     def exchange_yz(t):
         for x in range(16):
             send_y[t, 0, x : x + 1, :] = v[t, 1 + x, 8:9, :]
             send_y[t, 1, x : x + 1, :] = v[t, 1 + x, 39:40, :]
-        return [
-            push(send_z.at[t], recv_z.at[t, 1], (0, 0, -1)),
-            push(send_z.at[t], recv_z.at[t, 0], (0, 0, 1)),
-            push(send_y.at[t, 0], recv_y.at[t, 1], (0, -1, 0)),
-            push(send_y.at[t, 1], recv_y.at[t, 0], (0, 1, 0)),
-        ]
+        push(ROUND + t, send_z.at[t], recv_z.at[t, 1], (0, 0, -1))
+        push(ROUND + t, send_z.at[t], recv_z.at[t, 0], (0, 0, 1))
+        push(ROUND + t, send_y.at[t, 0], recv_y.at[t, 1], (0, -1, 0))
+        push(ROUND + t, send_y.at[t, 1], recv_y.at[t, 0], (0, 1, 0))
 
     def land(t):
         for x in range(16):
@@ -261,7 +273,7 @@
         total = total + (by[x] * v[t, 1 + x, 7:39, :] + hy[x] * v[t, 1 + x, 9:41, :])
         return c, total + (bz[x] * below + hz[x] * above)
 
-    received(faces)
+    received(FACES)
     bx[16] = next_x[...]
     ends = roll(next_z[...], -1, 1)
     packed = None
@@ -285,13 +297,10 @@
         v[0, 1 + x, 8:40, :] = g
         packed = pack_ends(packed, g, x)
         if x == 15:
-            rounds = [exchange_x(0)]
+            exchange_x(0)
     send_z[0] = packed
-    rounds[0] += exchange_yz(0)
-
-    coarsen(1, low, level_zero)
-    coarsen(2, low, own(1))
-    coarsen(3, low, own(2))
+    exchange_yz(0)
+
     coarsen(1, high, level_zero)
     coarsen(2, high, own(1))
     coarsen(3, high, own(2))
@@ -325,8 +334,7 @@
                 packed = jnp.where((lane16 == x) | (lane16 == x + 17), moved, packed)
         return packed
 
-    def send_one(s, p, r, q, reach):
-        copies = []
+    def send_one(group, s, p, r, q, reach):
         for d in BOX:
             if distance(d) not in reach:
                 continue
@@ -336,10 +344,9 @@
             ys = {0: pl.ds(0, 16), 1: pl.ds(12, 4), -1: pl.ds(0, 4)}[dy]
             yd = {0: pl.ds(0, 16), 1: pl.ds(20, 4), -1: pl.ds(16, 4)}[dy]
             if dz == 0:
-                copies.append(push(s.at[:, xs, ys], r.at[:, xd, yd], d))
+                push(group, s.at[:, xs, ys], r.at[:, xd, yd], d)
             else:
-                copies.append(push(p.at[:, ys], q.at[:, 0 if dz == 1 else 1, 1 - dx, yd], d))
-        return copies
+                push(group, p.at[:, ys], q.at[:, 0 if dz == 1 else 1, 1 - dx, yd], d)
 
     lane24 = iota((24, 128), 1)
 
@@ -356,7 +363,7 @@
         value = (fields[2 * f] + roll(fields[2 * f + 1], 64, 1)).reshape(8, 16, 128)
         s1c[f] = value
         r1c[f, 4:12, 0:16, :] = value
-    one_coefficients = send_one(s1c, p1c, r1c, q1c, (1,))
+    send_one(ONE_C, s1c, p1c, r1c, q1c, (1,))
 
     def pack_two(value):
         packed = value[0:8, :]
@@ -364,18 +371,16 @@
             packed = packed + roll(value[8 * x : 8 * x + 8, :], 32 * x, 1)
         return packed
 
-    def send_two(s, r, reach):
-        copies = []
+    def send_two(group, s, r, reach):
         for d in COLUMNS:
             if distance(d) not in reach:
                 continue
             target = r.at[1 - d[0], 1 if d[1] else 0, gz]
             if d[1] == 0:
-                copies.append(push(s, target, d))
+                push(group, s, target, d)
             else:
                 half = pl.ds(4, 4) if d[1] == 1 else pl.ds(0, 4)
-                copies.append(push(s.at[:, half], target.at[:, half], d))
-        return copies
+                push(group, s.at[:, half], target.at[:, half], d)
 
     def assemble_two(get, out):
         for b in range(3):
@@ -399,15 +404,15 @@
             v[t + 1, 1 + x, 8:40, :] = new
             packed = pack_ends(packed, new, x)
             if x == 15:
-                rounds.append(exchange_x(t + 1))
+                exchange_x(t + 1)
         send_z[t + 1] = packed
-        rounds[t + 1] += exchange_yz(t + 1)
-
-    sent(faces)
-    received(rounds[0])
+        exchange_yz(t + 1)
+
+    sent(FACES)
+    received(ROUND + 0)
     sweep(0)
 
-    one_coefficients += send_one(s1c, p1c, r1c, q1c, (2,))
+    send_one(ONE_C, s1c, p1c, r1c, q1c, (2,))
     for f, value in enumerate(own_coefficients(2)):
         s2c[f] = pack_two(value)
     r2c[1, 0, gz] = s2c[...]
@@ -420,11 +425,11 @@
     parity, chip = gy % 2, gy // 2
     r3[parity, chip, gz, gx] = total[0:4, :]
 
-    sent(rounds[0])
-    received(rounds[1])
+    sent(ROUND + 0)
+    received(ROUND + 1)
     sweep(1)
-    one_coefficients += send_one(s1c, p1c, r1c, q1c, (3,))
-    two_coefficients = send_two(s2c, r2c, (1, 2, 3))
+    send_one(ONE_C, s1c, p1c, r1c, q1c, (3,))
+    send_two(TWO_C, s2c, r2c, (1, 2, 3))
 
     def prepare(k, planes, scale):
         for x in range(planes):
@@ -435,26 +440,27 @@
             k[6, x] = roll(k[2, x], -1, 0)
             k[7, x] = roll(k[3, x], -1, 1)
 
-    sent(rounds[1])
-    received(rounds[2])
+    sent(ROUND + 1)
+    received(ROUND + 2)
     sweep(2)
-    two_coefficients += send_two(s2c, r2c, (4,))
+    send_two(TWO_C, s2c, r2c, (4,))
     block = r3.at[parity, chip, gz, gx]
-    three_x = [push(block, block, (d, 0, 0)) for d in (4, 3, 5, 2, 6, 1, 7)]
+    for d in (4, 3, 5, 2, 6, 1, 7):
+        push(THREE_X, block, block, (d, 0, 0))
 
     result = pltpu.make_async_copy(v.at[3, 1:17, 8:40], o0_h, out_sem)
     result.start()
 
-    received(one_coefficients)
+    received(ONE_C)
     for f in range(4):
         if f % 2 == 0:
             assemble_one(lambda x, f=f: r1c[f // 2, x], q1c, f, k1.at[f])
         else:
             assemble_one(lambda x, f=f: roll(r1c[f // 2, x], 64, 1), q1c, f, k1.at[f])
     prepare(k1, 16, 0.25)
-    sent(one_coefficients)
-    sent(rounds[2])
-    received(rounds[3])
+    sent(ONE_C)
+    sent(ROUND + 2)
+    received(ROUND + 3)
 
     ends = land(3)
     for x in range(0, 16, 2):
@@ -465,26 +471,28 @@
             pair = r if pair is None else pair + r
         fold[16 * x : 16 * x + 32, :] = pair
     value = fold[pl.ds(0, 128, stride=2), :] + fold[pl.ds(1, 128, stride=2), :]
-    value = dot(value, picker("pair", 0, 64, 64, 0.125))
+    value = dot(value, picker("pair", 0, 64, 64)) * 0.125
     s1s[0] = value.reshape(8, 16, 128)
     r1s[0, 4:12, 0:16, :] = s1s[0]
     p1s[0] = pack_one(value)
-    one_source = send_one(s1s, p1s, r1s, q1s, (1, 2, 3))
-
-    received(three_x)
+    send_one(ONE_S, s1s, p1s, r1s, q1s, (1, 2, 3))
+
+    received(THREE_X)
     block = r3.at[parity, chip, gz]
-    three_z = [push(block, block, (0, 0, d)) for d in (2, 1, 3)]
-    received(two_coefficients)
+    for d in (2, 1, 3):
+        push(THREE_Z, block, block, (0, 0, d))
+    received(TWO_C)
     for f in range(4):
         assemble_two(lambda b, t, z, f=f: r2c[b, t, z, f], k2.at[f])
     prepare(k2, 12, 0.25**2)
-    sent(two_coefficients)
-    sent(three_x)
-    received(three_z)
+    sent(TWO_C)
+    sent(THREE_X)
+    received(THREE_Z)
     block = r3.at[parity, chip]
-    three_y = [push(block, block, (0, d, 0)) for d in (4, 2, 6)]
-    sent(rounds[3])
-    received(one_source)
+    for d in (4, 2, 6):
+        push(THREE_Y, block, block, (0, d, 0))
+    sent(ROUND + 3)
+    received(ONE_S)
 
     def wide_around(k, c, lower, upper, x):
         total = k[1, x] * lower + k[1, x + 1] * upper
@@ -518,17 +526,17 @@
         r = wide_residual(k1, u1, 4 + 2 * x, 0.25) + wide_residual(k1, u1, 5 + 2 * x, 0.25)
         fold[16 * x : 16 * x + 16, :] = jnp.where(lane16 >= 64, r[0:16, :], 0.0)
     value = fold[pl.ds(0, 32, stride=2), :] + fold[pl.ds(1, 32, stride=2), :]
-    value = dot(value, picker("pair", 64, 32, 0, 0.125))
+    value = dot(value, picker("pair", 64, 32, 0)) * 0.125
     s2s[0] = pack_two(value)
     r2s[1, 0, gz] = s2s[...]
-    two_source = send_two(s2s, r2s, (1, 2, 3, 4))
-    sent(three_z)
-    received(three_y)
+    send_two(TWO_S, s2s, r2s, (1, 2, 3, 4))
+    sent(THREE_Z)
+    received(THREE_Y)
     block = r3.at[parity]
-    three_core = [push(block, block, None, (gx, gy + 1 - 2 * parity, gz))]
+    push(THREE_CORE, block, block, None, (gx, gy + 1 - 2 * parity, gz))
     for x in range(8):
         o1[x] = roll(u1[3, 4 + x, 0:16, :], 64, 1)[:, 0:64]
-    received(three_core)
+    received(THREE_CORE)
     group = (lane >> 4) & 3
     for x in range(8):
         for p in range(4):
@@ -547,9 +555,9 @@
         k3[7, x] = roll(k3[3, x], -1, 1)
         here, after = roll(k3[1, x], 64, 1), roll(k3[1, (x + 1) % 8], 64, 1)
         k3[10, x] = jnp.where(lane8 < 64, here, after)
-    sent(one_source)
-    sent(three_y)
-    received(two_source)
+    sent(ONE_S)
+    sent(THREE_Y)
+    received(TWO_S)
 
     assemble_two(lambda b, t, z: r2s[b, t, z, 0], k2.at[8])
     wide_level(k2, u2, 12)
@@ -557,16 +565,17 @@
         r = wide_residual(k2, u2, 4 + 2 * x, 0.25**2) + wide_residual(k2, u2, 5 + 2 * x, 0.25**2)
         fold[8 * x : 8 * x + 8, :] = r[0:8, :]
     value = fold[pl.ds(0, 8, stride=2), :] + fold[pl.ds(1, 8, stride=2), :]
-    value = dot(value, picker("pair", 0, 64, 0, 0.125))
+    value = dot(value, picker("pair", 0, 64, 0)) * 0.125
     halves = halves_of(value)
     s3s[...] = (halves + roll(halves, 4, 0))[0:4, :]
     r3s[gx, gy] = s3s[...]
-    three_source = [push(s3s, r3s.at[gx, gy], d) for d in PLANE]
+    for d in PLANE:
+        push(THREE_S, s3s, r3s.at[gx, gy], d)
     for x in range(4):
         o2[x] = roll(u2[3, 4 + x, 0:8, :], 128 - 32 * gz, 1)[:, 0:32]
-    sent(two_source)
-    sent(three_core)
-    received(three_source)
+    sent(TWO_S)
+    sent(THREE_CORE)
+    received(THREE_S)
 
     for y in range(8):
         k3[8, :, 4 * y : 4 * y + 4, :] = r3s[:, y]
@@ -599,12 +608,12 @@
         for y in range(8):
             x3[x, y, 0:4, :] = c[4 * y : 4 * y + 4, :]
     value = fold[pl.ds(0, 128, stride=2), :] + fold[pl.ds(1, 128, stride=2), :]
-    value = dot(value, picker("pair", 0, 32, 0, 0.125))
+    value = dot(value, picker("pair", 0, 32, 0)) * 0.125
     o4[...] = value.reshape(8, 16, 128)[:, :, 0:32]
     mine = x3[gx, gy]
     for half in range(2):
         o3[half] = roll(mine, (128 - 64 * half) - 16 * gz, 1)[0:4, 0:16]
-    sent(three_source)
+    sent(THREE_S)
     result.wait()
 
 
@@ -628,9 +637,9 @@
         vm(4, 8, 128), vm(1, 8, 128), vm(3, 2, 4, 4, 8, 128), vm(3, 2, 4, 1, 8, 128),
         vm(10, 12, 16, 128), vm(4, 12, 16, 128),
         vm(2, 4, 4, 8, 4, 128), vm(4, 128), vm(8, 8, 4, 128), vm(11, 8, 32, 128), vm(4, 8, 32, 128),
-        vm(8, 8, 8, 128),
+        vm(8, 8, 8, 128), vm(2048, 128),
         pltpu.SemaphoreType.DMA((5,)), pltpu.SemaphoreType.DMA,
-        pltpu.SemaphoreType.DMA((288,)), pltpu.SemaphoreType.DMA((288,)),
+        pltpu.SemaphoreType.DMA((GROUPS,)), pltpu.SemaphoreType.DMA((GROUPS,)),
     ]
     out = lambda *shape: jax.ShapeDtypeStruct(shape, F32)
     results = pl.pallas_call(

time: 56.3 us -> 51 us (0.906)
  Pallas kernels: 55.5 us -> 50.3 us
    pallas_call x1, Pallas kernels: 53.8 us -> 48.5 us  [body(): pl.pallas_call(kernel, out_shape=(out(16, 32, 128), out(8, 16, 64), out(4...]
where the time goes in v3:
time: 51 us; the launch traced here: 50.9 us
  Pallas kernels  50.3 us (99%)
  between operations  0.64 us (1%)
    pallas_call x1, Pallas kernels, body(): pl.pallas_call(kernel, out_shape=(out(16, 32, 128), out(8, 16, 64), out(4...  48.5 us
    pallas_call x1, Pallas kernels, body(): pl.pallas_call(hand_over, out_shape=tuple((out(*r.shape) for r in results...  1.75 us

profile of v3, /device:TPU:1, one launch (start us, length us, event | category | flops | bytes accessed | tf_op | source)
XLA Modules:
  0.0 50.9 jit_solution(1431686794352089604)
XLA Ops:
  0.6 48.5 %shard_map.92 = (f32[16,32,128]{2,1,0:T(8,128)}, f32[8,16,64]{2,1,0:T(8,128)}, f32[4,8,32]{2,1,0:T(8,128)}, f32[2,4,16]{2,1,0:T(4,128)}, f32[8,16,32]{2,1,0:T(8,128)}) custom-call(f32[16,32,128]{2,1,0:T(8,128)} %src_h.1, f32[16,32,128]{2,1,0:T(8,128)} %a_h.1, f32[16,32,128]{2,1,0:T(8,128)} %bx_h.1, f32[16,32,128]{2,1,0:T(8,128)} %by_h.1, f32[16,32,128]{2,1,0:T(8,128)} %bz_h.1), custom_call_target="tpu_custom_call" | custom-call | tf_op jit(solution)/shard_map/pallas_call | solution.py:645
  49.1 1.8 %shard_map.93 = (f32[16,32,128]{2,1,0:T(8,128)}, f32[8,16,64]{2,1,0:T(8,128)}, f32[4,8,32]{2,1,0:T(8,128)}, f32[2,4,16]{2,1,0:T(4,128)}, f32[8,16,32]{2,1,0:T(8,128)}) custom-call(f32[16,32,128]{2,1,0:T(8,128)} %get-tuple-element.10.refs_0_, f32[8,16,64]{2,1,0:T(8,128)} %get-tuple-element.11.refs_1_, f32[4,8,32]{2,1,0:T(8,128)} %get-tuple-element.12.refs_2_, ...), custom_call_target="tpu_custom_call" | custom-call | tf_op jit(solution)/shard_map/pallas_call | solution.py:655

commit v4 on v3

--- a/solution.py
+++ b/solution.py
@@ -187,6 +187,15 @@
         send_fy[x : x + 1, :] = by[x, 0:1, :] * inner_y
         packed = pack_ends(packed, bz[x], x)
     send_fz[...] = packed * inner_z
+
+    zeros = jnp.zeros((32, 128), F32)
+    v[3, 0, 8:40, :] = zeros
+    v[3, 17, 8:40, :] = zeros
+    for x in range(16):
+        v[3, 1 + x, 7:8, :] = zeros[0:1, :]
+        v[3, 1 + x, 40:41, :] = zeros[0:1, :]
+    for e in range(10):
+        s1s[e] = zeros[0:24, :]
 
     SHAPES = {1: (16, 32), 2: (8, 16), 3: (4, 8)}
     LANES = {1: (0, 64, 64), 2: (64, 32, 0), 3: (0, 16, 0)}
@@ -266,7 +275,7 @@
 
     def around(t, x, ends):
         c = v[t, 1 + x, 8:40, :]
-        halo = unpack_ends(ends, x)
+        halo = 0.0 if ends is None else unpack_ends(ends, x)
         below = jnp.where(lane32 == 0, halo, roll(c, 1, 1))
         above = jnp.where(lane32 == 127, halo, roll(c, -1, 1))
         total = bx[x] * v[t, x, 8:40, :] + bx[x + 1] * v[t, x + 2, 8:40, :]
@@ -342,7 +351,7 @@
             xs = {0: pl.ds(0, 8), 1: pl.ds(4, 4), -1: pl.ds(0, 4)}[dx]
             xd = {0: pl.ds(4, 8), 1: pl.ds(0, 4), -1: pl.ds(12, 4)}[dx]
             ys = {0: pl.ds(0, 16), 1: pl.ds(12, 4), -1: pl.ds(0, 4)}[dy]
-            yd = {0: pl.ds(0, 16), 1: pl.ds(20, 4), -1: pl.ds(16, 4)}[dy]
+            yd = {0: pl.ds(4, 16), 1: pl.ds(0, 4), -1: pl.ds(20, 4)}[dy]
             if dz == 0:
                 push(group, s.at[:, xs, ys], r.at[:, xd, yd], d)
             else:
@@ -362,7 +371,7 @@
     for f in range(2):
         value = (fields[2 * f] + roll(fields[2 * f + 1], 64, 1)).reshape(8, 16, 128)
         s1c[f] = value
-        r1c[f, 4:12, 0:16, :] = value
+        r1c[f, 4:12, 4:20, :] = value
     send_one(ONE_C, s1c, p1c, r1c, q1c, (1,))
 
     def pack_two(value):
@@ -402,11 +411,14 @@
             if t > 0:
                 new = new - momentum * v[t - 1, 1 + x, 8:40, :]
             v[t + 1, 1 + x, 8:40, :] = new
+            if t == 2:
+                continue
             packed = pack_ends(packed, new, x)
             if x == 15:
                 exchange_x(t + 1)
-        send_z[t + 1] = packed
-        exchange_yz(t + 1)
+        if t < 2:
+            send_z[t + 1] = packed
+            exchange_yz(t + 1)
 
     sent(FACES)
     received(ROUND + 0)
@@ -423,7 +435,10 @@
         halves = roll(halves + roll(halves, 4, 0), 16 * f, 1)
         total = halves if total is None else total + halves
     parity, chip = gy % 2, gy // 2
-    r3[parity, chip, gz, gx] = total[0:4, :]
+    r3[parity, chip, gx, gz] = total[0:4, :]
+    block = r3.at[parity, chip, gx, gz]
+    for d in (2, 1, 3):
+        push(THREE_Z, block, block, (0, 0, d))
 
     sent(ROUND + 0)
     received(ROUND + 1)
@@ -440,14 +455,60 @@
             k[6, x] = roll(k[2, x], -1, 0)
             k[7, x] = roll(k[3, x], -1, 1)
 
+    received(THREE_Z)
+    sent(THREE_Z)
     sent(ROUND + 1)
     received(ROUND + 2)
     sweep(2)
+
+    for x in range(0, 16, 2):
+        pair, ends = None, None
+        for y in (x, x + 1):
+            c, total = around(3, y, None)
+            r = (src[y] - diag[y] * c) + total
+            e = jnp.where(lane32 == 127, hz[y] * c, jnp.where(lane32 == 0, bz[y] * c, 0.0))
+            pair = r if pair is None else pair + r
+            ends = e if ends is None else ends + e
+            fold[320 + y : 321 + y, :] = by[y, 0:1, :] * c[0:1, :]
+            fold[336 + y : 337 + y, :] = hy[y, 31:32, :] * c[31:32, :]
+        fold[16 * x : 16 * x + 32, :] = pair
+        tmp[16 * x : 16 * x + 32, :] = ends
+    fold[256:288, :] = bx[0] * v[3, 1, 8:40, :]
+    fold[288:320, :] = bx[16] * v[3, 16, 8:40, :]
+    value = fold[pl.ds(0, 176, stride=2), :] + fold[pl.ds(1, 176, stride=2), :]
+    value = dot(value, picker("pair", 0, 64, 64)) * 0.125
+    ends = (tmp[pl.ds(0, 128, stride=2), :] + tmp[pl.ds(1, 128, stride=2), :]) * 0.125
+    lane128 = iota((128, 128), 1)
+    ends = jnp.where(lane128 == 0, roll(ends, 1, 1), jnp.where(lane128 == 63, roll(ends, 63, 1), 0.0))
+    own_block = value[0:128, :] + ends
+    for x in range(8):
+        s1s[1 + x, 4:20, :] = own_block[16 * x : 16 * x + 16, :]
+        s1s[1 + x, 3:4, :] = value[160 + x : 161 + x, :]
+        s1s[1 + x, 20:21, :] = value[168 + x : 169 + x, :]
+    s1s[0, 4:20, :] = value[128:144, :]
+    s1s[9, 4:20, :] = value[144:160, :]
+    packed = jnp.zeros((24, 128), F32)
+    for e in range(10):
+        low_group = (lane24 >= 5 * e) & (lane24 < 5 * e + 5)
+        high_group = (lane24 >= 5 * e + 67) & (lane24 < 5 * e + 72)
+        packed = jnp.where(low_group | high_group, roll(s1s[e], 5 * e + 4, 1), packed)
+    p1s[...] = packed
+    for d in BOX:
+        dx, dy, dz = d
+        es = {0: pl.ds(0, 10), 1: pl.ds(5, 5), -1: pl.ds(0, 5)}[dx]
+        ys = {0: pl.ds(0, 24), 1: pl.ds(16, 8), -1: pl.ds(0, 8)}[dy]
+        yd = {0: pl.ds(0, 24), 1: pl.ds(24, 8), -1: pl.ds(32, 8)}[dy]
+        if dz == 0:
+            push(ONE_S, s1s.at[es, ys], r1s.at[1 - dx, es, yd], d)
+        else:
+            push(ONE_S, p1s.at[ys], q1s.at[0 if dz == 1 else 1, 1 - dx, yd], d)
+    for e in range(10):
+        r1s[1, e, 0:24, :] = s1s[e]
+
     send_two(TWO_C, s2c, r2c, (4,))
-    block = r3.at[parity, chip, gz, gx]
+    block = r3.at[parity, chip, gx]
     for d in (4, 3, 5, 2, 6, 1, 7):
         push(THREE_X, block, block, (d, 0, 0))
-
     result = pltpu.make_async_copy(v.at[3, 1:17, 8:40], o0_h, out_sem)
     result.start()
 
@@ -460,38 +521,6 @@
     prepare(k1, 16, 0.25)
     sent(ONE_C)
     sent(ROUND + 2)
-    received(ROUND + 3)
-
-    ends = land(3)
-    for x in range(0, 16, 2):
-        pair = None
-        for y in (x, x + 1):
-            c, total = around(3, y, ends)
-            r = (src[y] - diag[y] * c) + total
-            pair = r if pair is None else pair + r
-        fold[16 * x : 16 * x + 32, :] = pair
-    value = fold[pl.ds(0, 128, stride=2), :] + fold[pl.ds(1, 128, stride=2), :]
-    value = dot(value, picker("pair", 0, 64, 64)) * 0.125
-    s1s[0] = value.reshape(8, 16, 128)
-    r1s[0, 4:12, 0:16, :] = s1s[0]
-    p1s[0] = pack_one(value)
-    send_one(ONE_S, s1s, p1s, r1s, q1s, (1, 2, 3))
-
-    received(THREE_X)
-    block = r3.at[parity, chip, gz]
-    for d in (2, 1, 3):
-        push(THREE_Z, block, block, (0, 0, d))
-    received(TWO_C)
-    for f in range(4):
-        assemble_two(lambda b, t, z, f=f: r2c[b, t, z, f], k2.at[f])
-    prepare(k2, 12, 0.25**2)
-    sent(TWO_C)
-    sent(THREE_X)
-    received(THREE_Z)
-    block = r3.at[parity, chip]
-    for d in (4, 2, 6):
-        push(THREE_Y, block, block, (0, d, 0))
-    sent(ROUND + 3)
     received(ONE_S)
 
     def wide_around(k, c, lower, upper, x):
@@ -519,28 +548,71 @@
         total = wide_around(k, c, u[3, x - 1], u[3, x + 1], x)
         return (k[8, x] - k[0, x] * c) + scale * total
 
-    assemble_one(lambda x: r1s[0, x], q1s, 0, k1.at[8])
+    def overlap(value):
+        return jnp.concatenate(
+            [value[0:8] + value[24:32], value[8:16], value[16:24] + value[32:40]], axis=0
+        )
+
+    middle_lanes = (lane24 >= 63) | (lane24 == 0)
+    side_lanes = ((lane24 >= 60) & (lane24 <= 64)) | (lane24 <= 3) | (lane24 == 127)
+    lane40 = iota((40, 128), 1)
+    sides = [overlap(jnp.where(lane40 < 58, q1s[0, b], q1s[1, b])) for b in range(3)]
+    for x in range(16):
+        total = None
+        for b, e in ((1, x - 3), (2, x - 11), (0, x + 5)):
+            if not (5 if b == 0 else 0) <= e <= (4 if b == 2 else 9):
+                continue
+            part = jnp.where(middle_lanes, overlap(r1s[b, e]), 0.0)
+            part = part + jnp.where(side_lanes, roll(sides[b], 60 - 5 * e, 1), 0.0)
+            total = part if total is None else total + part
+        k1[8, x] = total
     wide_level(k1, u1, 16)
     lane16 = iota((16, 128), 1)
     for x in range(4):
         r = wide_residual(k1, u1, 4 + 2 * x, 0.25) + wide_residual(k1, u1, 5 + 2 * x, 0.25)
-        fold[16 * x : 16 * x + 16, :] = jnp.where(lane16 >= 64, r[0:16, :], 0.0)
+        fold[16 * x : 16 * x + 16, :] = jnp.where(lane16 >= 64, r[4:20, :], 0.0)
     value = fold[pl.ds(0, 32, stride=2), :] + fold[pl.ds(1, 32, stride=2), :]
     value = dot(value, picker("pair", 64, 32, 0)) * 0.125
     s2s[0] = pack_two(value)
     r2s[1, 0, gz] = s2s[...]
     send_two(TWO_S, s2s, r2s, (1, 2, 3, 4))
-    sent(THREE_Z)
+    for x in range(8):
+        o1[x] = roll(u1[3, 4 + x, 4:20, :], 64, 1)[:, 0:64]
+    received(THREE_X)
+    block = r3.at[parity, chip]
+    for d in (4, 2, 6):
+        push(THREE_Y, block, block, (0, d, 0))
+    sent(THREE_X)
+    sent(TWO_C)
+    received(TWO_C)
+    for f in range(4):
+        assemble_two(lambda b, t, z, f=f: r2c[b, t, z, f], k2.at[f])
+    prepare(k2, 12, 0.25**2)
+    sent(ONE_S)
+    received(TWO_S)
+
+    assemble_two(lambda b, t, z: r2s[b, t, z, 0], k2.at[8])
+    wide_level(k2, u2, 12)
+    for x in range(2):
+        r = wide_residual(k2, u2, 4 + 2 * x, 0.25**2) + wide_residual(k2, u2, 5 + 2 * x, 0.25**2)
+        fold[8 * x : 8 * x + 8, :] = r[0:8, :]
+    value = fold[pl.ds(0, 8, stride=2), :] + fold[pl.ds(1, 8, stride=2), :]
+    value = dot(value, picker("pair", 0, 64, 0)) * 0.125
+    halves = halves_of(value)
+    s3s[...] = (halves + roll(halves, 4, 0))[0:4, :]
+    r3s[gx, gy] = s3s[...]
+    for d in PLANE:
+        push(THREE_S, s3s, r3s.at[gx, gy], d)
+    for x in range(4):
+        o2[x] = roll(u2[3, 4 + x, 0:8, :], 128 - 32 * gz, 1)[:, 0:32]
     received(THREE_Y)
     block = r3.at[parity]
     push(THREE_CORE, block, block, None, (gx, gy + 1 - 2 * parity, gz))
-    for x in range(8):
-        o1[x] = roll(u1[3, 4 + x, 0:16, :], 64, 1)[:, 0:64]
     received(THREE_CORE)
     group = (lane >> 4) & 3
     for x in range(8):
         for p in range(4):
-            tiles = [jnp.concatenate([r3[0, p, z, x], r3[1, p, z, x]], axis=0) for z in range(4)]
+            tiles = [jnp.concatenate([r3[0, p, x, z], r3[1, p, x, z]], axis=0) for z in range(4)]
             for f in range(4):
                 value = roll(tiles[0], -16 * f, 1)
                 for z in range(1, 4):
@@ -555,25 +627,8 @@
         k3[7, x] = roll(k3[3, x], -1, 1)
         here, after = roll(k3[1, x], 64, 1), roll(k3[1, (x + 1) % 8], 64, 1)
         k3[10, x] = jnp.where(lane8 < 64, here, after)
-    sent(ONE_S)
+    sent(TWO_S)
     sent(THREE_Y)
-    received(TWO_S)
-
-    assemble_two(lambda b, t, z: r2s[b, t, z, 0], k2.at[8])
-    wide_level(k2, u2, 12)
-    for x in range(2):
-        r = wide_residual(k2, u2, 4 + 2 * x, 0.25**2) + wide_residual(k2, u2, 5 + 2 * x, 0.25**2)
-        fold[8 * x : 8 * x + 8, :] = r[0:8, :]
-    value = fold[pl.ds(0, 8, stride=2), :] + fold[pl.ds(1, 8, stride=2), :]
-    value = dot(value, picker("pair", 0, 64, 0)) * 0.125
-    halves = halves_of(value)
-    s3s[...] = (halves + roll(halves, 4, 0))[0:4, :]
-    r3s[gx, gy] = s3s[...]
-    for d in PLANE:
-        push(THREE_S, s3s, r3s.at[gx, gy], d)
-    for x in range(4):
-        o2[x] = roll(u2[3, 4 + x, 0:8, :], 128 - 32 * gz, 1)[:, 0:32]
-    sent(TWO_S)
     sent(THREE_CORE)
     received(THREE_S)
 
@@ -630,13 +685,13 @@
         vm(4, 18, 48, 128),
         vm(32, 128), vm(16, 128), vm(8, 128), vm(32, 128), vm(16, 128), vm(8, 128),
         vm(4, 2, 16, 128), vm(4, 2, 8, 128), vm(4, 2, 16, 128), vm(4, 8, 128),
-        vm(256, 128), vm(256, 128),
-        vm(2, 8, 16, 128), vm(4, 16, 128), vm(1, 8, 16, 128), vm(1, 16, 128),
-        vm(2, 16, 24, 128), vm(4, 2, 3, 24, 128), vm(1, 16, 24, 128), vm(1, 2, 3, 24, 128),
+        vm(256, 128), vm(352, 128),
+        vm(2, 8, 16, 128), vm(4, 16, 128), vm(10, 24, 128), vm(24, 128),
+        vm(2, 16, 24, 128), vm(4, 2, 3, 24, 128), vm(3, 10, 40, 128), vm(2, 3, 40, 128),
         vm(10, 16, 24, 128), vm(4, 16, 24, 128),
         vm(4, 8, 128), vm(1, 8, 128), vm(3, 2, 4, 4, 8, 128), vm(3, 2, 4, 1, 8, 128),
         vm(10, 12, 16, 128), vm(4, 12, 16, 128),
-        vm(2, 4, 4, 8, 4, 128), vm(4, 128), vm(8, 8, 4, 128), vm(11, 8, 32, 128), vm(4, 8, 32, 128),
+        vm(2, 4, 8, 4, 4, 128), vm(4, 128), vm(8, 8, 4, 128), vm(11, 8, 32, 128), vm(4, 8, 32, 128),
         vm(8, 8, 8, 128), vm(2048, 128),
         pltpu.SemaphoreType.DMA((5,)), pltpu.SemaphoreType.DMA,
         pltpu.SemaphoreType.DMA((GROUPS,)), pltpu.SemaphoreType.DMA((GROUPS,)),

time: 51 us -> 47.9 us (0.939)
  Pallas kernels: 50.3 us -> 47.1 us
    pallas_call x1, Pallas kernels: 48.5 us -> 45.4 us  [body(): pl.pallas_call(kernel, out_shape=(out(16, 32, 128), out(8, 16, 64), out(4...]
where the time goes in v4:
time: 47.9 us; the launch traced here: 47.8 us
  Pallas kernels  47.1 us (98%)
  between operations  0.64 us (1%)
    pallas_call x1, Pallas kernels, body(): pl.pallas_call(kernel, out_shape=(out(16, 32, 128), out(8, 16, 64), out(4...  45.4 us
    pallas_call x1, Pallas kernels, body(): pl.pallas_call(hand_over, out_shape=tuple((out(*r.shape) for r in results...  1.75 us

profile of v4, /device:TPU:1, one launch (start us, length us, event | category | flops | bytes accessed | tf_op | source)
XLA Modules:
  0.0 47.8 jit_solution(10778446855763370558)
XLA Ops:
  0.6 45.4 %shard_map.92 = (f32[16,32,128]{2,1,0:T(8,128)}, f32[8,16,64]{2,1,0:T(8,128)}, f32[4,8,32]{2,1,0:T(8,128)}, f32[2,4,16]{2,1,0:T(4,128)}, f32[8,16,32]{2,1,0:T(8,128)}) custom-call(f32[16,32,128]{2,1,0:T(8,128)} %src_h.1, f32[16,32,128]{2,1,0:T(8,128)} %a_h.1, f32[16,32,128]{2,1,0:T(8,128)} %bx_h.1, f32[16,32,128]{2,1,0:T(8,128)} %by_h.1, f32[16,32,128]{2,1,0:T(8,128)} %bz_h.1), custom_call_target="tpu_custom_call" | custom-call | tf_op jit(solution)/shard_map/pallas_call | solution.py:700
  46.0 1.8 %shard_map.93 = (f32[16,32,128]{2,1,0:T(8,128)}, f32[8,16,64]{2,1,0:T(8,128)}, f32[4,8,32]{2,1,0:T(8,128)}, f32[2,4,16]{2,1,0:T(4,128)}, f32[8,16,32]{2,1,0:T(8,128)}) custom-call(f32[16,32,128]{2,1,0:T(8,128)} %get-tuple-element.10.refs_0_, f32[8,16,64]{2,1,0:T(8,128)} %get-tuple-element.11.refs_1_, f32[4,8,32]{2,1,0:T(8,128)} %get-tuple-element.12.refs_2_, ...), custom_call_target="tpu_custom_call" | custom-call | tf_op jit(solution)/shard_map/pallas_call | solution.py:710

commit v5 on v4

--- a/solution.py
+++ b/solution.py
@@ -29,7 +29,7 @@
 SIX = tuple(d for d in BOX if distance(d) == 1)
 
 FACES, ROUND, ONE_C, ONE_S, TWO_C, TWO_S = 0, 1, 5, 6, 7, 8
-THREE_X, THREE_Z, THREE_Y, THREE_CORE, THREE_S, GROUPS = 9, 10, 11, 12, 13, 14
+THREE_X, THREE_Z, THREE_Y, THREE_CORE, THREE_S, ROUND_X, GROUPS = 9, 10, 11, 12, 13, 14, 18
 
 FIELDS = (
     ("a", "pair", "pair", "pair"),
@@ -151,7 +151,7 @@
         wait(group, send_sem)
 
     barrier = pltpu.get_barrier_semaphore()
-    for d in SIX:
+    for d in ((1, 0, 0), (0, 1, 0), (0, 0, 1)):
         pl.semaphore_signal(barrier, inc=1, device_id=neighbour(d), device_id_type=MESH)
 
     loads = []
@@ -242,7 +242,7 @@
     coarsen(2, low, own(1))
     coarsen(3, low, own(2))
 
-    pl.semaphore_wait(barrier, 6)
+    pl.semaphore_wait(barrier, 3)
 
     push(FACES, send_fx, next_x, (-1, 0, 0))
     push(FACES, send_fy, next_y, (0, -1, 0))
@@ -255,8 +255,8 @@
     ORDER = (0, 15) + tuple(range(1, 15))
 
     def exchange_x(t):
-        push(ROUND + t, v.at[t, 1, 8:40], v.at[t, 17, 8:40], (-1, 0, 0))
-        push(ROUND + t, v.at[t, 16, 8:40], v.at[t, 0, 8:40], (1, 0, 0))
+        push(ROUND_X + t, v.at[t, 1, 8:40], v.at[t, 17, 8:40], (-1, 0, 0))
+        push(ROUND_X + t, v.at[t, 16, 8:40], v.at[t, 0, 8:40], (1, 0, 0))
 
     def exchange_yz(t):
         for x in range(16):
@@ -403,9 +403,12 @@
 
     def sweep(t):
         momentum, step = WEIGHTS[t + 1]
+        received(ROUND + t)
         ends = land(t)
         packed = None
-        for x in ORDER:
+        for x in tuple(range(1, 15)) + (0, 15):
+            if x == 0:
+                received(ROUND_X + t)
             c, total = around(t, x, ends)
             new = (1.0 + momentum - step) * c + step * (gain[x] + inv_s[x] * total)
             if t > 0:
@@ -414,14 +417,12 @@
             if t == 2:
                 continue
             packed = pack_ends(packed, new, x)
-            if x == 15:
-                exchange_x(t + 1)
         if t < 2:
+            exchange_x(t + 1)
             send_z[t + 1] = packed
             exchange_yz(t + 1)
 
     sent(FACES)
-    received(ROUND + 0)
     sweep(0)
 
     send_one(ONE_C, s1c, p1c, r1c, q1c, (2,))
@@ -441,7 +442,7 @@
         push(THREE_Z, block, block, (0, 0, d))
 
     sent(ROUND + 0)
-    received(ROUND + 1)
+    sent(ROUND_X + 0)
     sweep(1)
     send_one(ONE_C, s1c, p1c, r1c, q1c, (3,))
     send_two(TWO_C, s2c, r2c, (1, 2, 3))
@@ -458,7 +459,7 @@
     received(THREE_Z)
     sent(THREE_Z)
     sent(ROUND + 1)
-    received(ROUND + 2)
+    sent(ROUND_X + 1)
     sweep(2)
 
     for x in range(0, 16, 2):
@@ -521,6 +522,7 @@
     prepare(k1, 16, 0.25)
     sent(ONE_C)
     sent(ROUND + 2)
+    sent(ROUND_X + 2)
     received(ONE_S)
 
     def wide_around(k, c, lower, upper, x):

time: 47.9 us -> 48 us (level)
  no operation moved by 1% of the time
where the time goes in v5:
time: 48 us; the launch traced here: 47.9 us
  Pallas kernels  47.2 us (98%)
  between operations  0.64 us (1%)
    pallas_call x1, Pallas kernels, body(): pl.pallas_call(kernel, out_shape=(out(16, 32, 128), out(8, 16, 64), out(4...  45.5 us
    pallas_call x1, Pallas kernels, body(): pl.pallas_call(hand_over, out_shape=tuple((out(*r.shape) for r in results...  1.75 us

profile of v5, /device:TPU:1, one launch (start us, length us, event | category | flops | bytes accessed | tf_op | source)
XLA Modules:
  0.0 47.9 jit_solution(3030517398370677964)
XLA Ops:
  0.6 45.5 %shard_map.92 = (f32[16,32,128]{2,1,0:T(8,128)}, f32[8,16,64]{2,1,0:T(8,128)}, f32[4,8,32]{2,1,0:T(8,128)}, f32[2,4,16]{2,1,0:T(4,128)}, f32[8,16,32]{2,1,0:T(8,128)}) custom-call(f32[16,32,128]{2,1,0:T(8,128)} %src_h.1, f32[16,32,128]{2,1,0:T(8,128)} %a_h.1, f32[16,32,128]{2,1,0:T(8,128)} %bx_h.1, f32[16,32,128]{2,1,0:T(8,128)} %by_h.1, f32[16,32,128]{2,1,0:T(8,128)} %bz_h.1), custom_call_target="tpu_custom_call" | custom-call | tf_op jit(solution)/shard_map/pallas_call | solution.py:702
  46.1 1.8 %shard_map.93 = (f32[16,32,128]{2,1,0:T(8,128)}, f32[8,16,64]{2,1,0:T(8,128)}, f32[4,8,32]{2,1,0:T(8,128)}, f32[2,4,16]{2,1,0:T(4,128)}, f32[8,16,32]{2,1,0:T(8,128)}) custom-call(f32[16,32,128]{2,1,0:T(8,128)} %get-tuple-element.10.refs_0_, f32[8,16,64]{2,1,0:T(8,128)} %get-tuple-element.11.refs_1_, f32[4,8,32]{2,1,0:T(8,128)} %get-tuple-element.12.refs_2_, ...), custom_call_target="tpu_custom_call" | custom-call | tf_op jit(solution)/shard_map/pallas_call | solution.py:712
